TPU v7x, 32 devices: a whole 2x2x4 slice. The times are simulated.
32 devices in a mesh: row: 8 (over z, x), col: 4 (over y, core).
Axes of the slice: x: 2, y: 2, z: 4, core: 2. Of those that a mesh axis runs over, the one named last changes fastest.
Arguments:
- tokens: bfloat16 [4096, 4096], P('row', 'col'), may hold values from -6 to 6
- gate_weight: bfloat16 [4096, 16384], P('row', 'col'), may hold values from -0.125 to 0.125
- up_weight: bfloat16 [4096, 16384], P('row', 'col'), may hold values from -0.125 to 0.125
- tile_mask: int32 [32, 128], P(None, 'col'), may hold values from 0 to 1, as said below
Outputs:
- hidden: bfloat16 [4096, 16384], P('row', 'col')
Inputs may be any that keep to these rules, and one draw needn't show every extreme that they name: `tile_mask`: values are 0 or 1. In each aligned block of 4 x 32 tiles (tile rows r * 4 to (r + 1) * 4 - 1, tile columns c * 32 to (c + 1) * 32 - 1) at least 48 and at most 80 tiles are kept; some block keeps exactly 80.
All inputs are finite; a program needn't handle non-finite values.
Results may differ from a plain program's by a relative error of at most 0.001.
Values may be sent and summed in bfloat16 or wider, within the bound.
A program may use at most 128 MiB of HBM per device.

v0:
```python
import functools

import jax
import jax.numpy as jnp
from jax import lax
from jax.experimental import pallas as pl
from jax.experimental.pallas import tpu as pltpu
from jax.sharding import PartitionSpec as P

TILE = 128
VMEM_LIMIT = 56 * 1024 * 1024


def pack_kernel(row_tiles, col_tiles, core_ref, mask_ref, gate_ref, up_ref, mine_ref, other_ref):
    core = core_ref[0]

    def tile_step(i, j, slot):
        kept = mask_ref[i * col_tiles + j]
        rows = pl.ds(i * TILE, TILE)
        cols = pl.ds(pl.multiple_of(j * TILE, TILE), TILE)

        @pl.when((kept == 1) & (core == 0))
        def _():
            mine_ref[slot] = gate_ref[rows, cols]
            other_ref[slot] = up_ref[rows, cols]

        @pl.when((kept == 1) & (core == 1))
        def _():
            mine_ref[slot] = up_ref[rows, cols]
            other_ref[slot] = gate_ref[rows, cols]

        return slot + kept

    slot = jnp.int32(0)
    for i in range(row_tiles):
        slot = lax.fori_loop(0, col_tiles, functools.partial(tile_step, i), slot)


def block_kernel(row_tiles, col_tiles, chunk_tiles, counts, first, last, codes_ref, info_ref, *rest):
    blocks = len(counts)
    tok_refs, rest = rest[:blocks], rest[blocks:]
    pieces, rest = rest[:2 * sum(counts)], rest[2 * sum(counts):]
    if first:
        acc_ref = None
    else:
        acc_ref, rest = rest[0], rest[1:]
    out_ref, packed, dense, sems = rest
    core = info_ref[blocks]
    chunk = pl.program_id(0)

    @pl.when(chunk == 0)
    def _():
        copies = []
        for b in range(blocks):
            for kind in range(2):
                start = 0
                for _ in range(counts[b]):
                    ref = pieces[len(copies)]
                    copies.append(pltpu.make_async_copy(
                        ref, packed.at[b, kind, pl.ds(start, ref.shape[0])], sems.at[len(copies)]))
                    start += ref.shape[0]
        for copy in copies:
            copy.start()
        for copy in copies:
            copy.wait()

    sums = []
    for kind in range(2):
        total = None if first else acc_ref[kind]
        for b in range(blocks):
            for i in range(row_tiles):
                for j in range(chunk_tiles):
                    code = codes_ref[(info_ref[b] * row_tiles + i) * col_tiles + chunk * chunk_tiles + j]
                    tile = packed[b, kind, jnp.maximum(code, 0)]
                    dense[b, kind, pl.ds(i * TILE, TILE), pl.ds(j * TILE, TILE)] = jnp.where(
                        code >= 0, tile, jnp.zeros_like(tile))
            product = jnp.dot(tok_refs[b][...], dense[b, kind], preferred_element_type=jnp.float32)
            total = product if total is None else total + product
        if last:
            sums.append(total)
        else:
            out_ref[kind] = total
    if last:
        gate = jnp.where(core == 0, sums[0], sums[1])
        up = jnp.where(core == 0, sums[1], sums[0])
        out_ref[...] = (gate / (1.0 + jnp.exp(-gate)) * up).astype(out_ref.dtype)


def solution(mesh):
    R, C = mesh.shape["row"], mesh.shape["col"]
    NZ = R // 2
    axes = ("row", "col")

    def send(value, move):
        pairs = []
        for r in range(R):
            for c in range(C):
                tr, tc = move(r, c)
                pairs.append((r * C + c, tr * C + tc))
        return lax.ppermute(value, axes, pairs)

    sibling = lambda r, c: (r, c ^ 1)
    z_pair = lambda r, c: (r ^ 2, c)
    x_pair = lambda r, c: (r ^ 1, c)

    def swap_out(r, c):
        return (r, c) if ((r // 2) % 2) == (c % 2) else (r ^ 2, c ^ 1)

    def on_device(tokens, gate_weight, up_weight, tile_mask):
        depth, cols = gate_weight.shape
        row_tiles, col_tiles = depth // TILE, cols // TILE
        slots = 5 * row_tiles * col_tiles // 8
        rows = tokens.shape[0]
        r = lax.axis_index("row")
        core = lax.axis_index("col") % 2
        home = ((r // 2) % 2) == core

        def after(value, acc):
            return lax.optimization_barrier((value, acc))

        tok_other = send(tokens, z_pair)
        smem = pl.BlockSpec(memory_space=pltpu.SMEM)
        vmem = pl.BlockSpec(memory_space=pltpu.VMEM)
        own_mask = lax.dynamic_slice_in_dim(tile_mask, r * row_tiles, row_tiles, 0).reshape(-1)
        piece = jax.ShapeDtypeStruct((slots, TILE, TILE), gate_weight.dtype)
        mine, other = pl.pallas_call(
            functools.partial(pack_kernel, row_tiles, col_tiles),
            out_shape=(piece, piece),
            in_specs=[smem, smem, vmem, vmem],
            out_specs=(vmem, vmem),
            compiler_params=pltpu.CompilerParams(vmem_limit_bytes=VMEM_LIMIT),
            name="pack",
        )(core.reshape(1).astype(jnp.int32), own_mask, gate_weight, up_weight)

        mask_sib = send(tile_mask, sibling)
        job_mask = jnp.where(home, tile_mask, mask_sib).reshape(R, row_tiles * col_tiles)
        place = jnp.arange(row_tiles * col_tiles)
        upto = (place[None, :] <= place[:, None]).astype(jnp.int32)
        slot = jnp.sum(job_mask[:, None, :] * upto[None], axis=2) - 1
        codes = jnp.where(job_mask == 1, slot, -1).reshape(-1)

        crossed, tok_other = after(send(other, sibling), tok_other)
        keep = jnp.where(home, mine, crossed)
        give = jnp.where(home, crossed, mine)
        chunk_tiles = min(4, col_tiles)
        width = chunk_tiles * TILE

        def add_blocks(acc, todo, last=False):
            first = acc is None
            counts = tuple(len(values) for values, _ in todo)
            info = jnp.stack([block for _, block in todo] + [core]).astype(jnp.int32)
            acc_spec = pl.BlockSpec((2, rows, width), lambda g, *_: (0, 0, g))
            in_specs = [pl.BlockSpec((rows, depth), lambda g, codes, info, b=b: (0, info[b]))
                        for b in range(len(todo))]
            operands = [codes, info] + [tok] * len(todo)
            for values, _ in todo:
                operands += [v for v, _ in values] + [w for _, w in values]
            in_specs += [pl.BlockSpec(memory_space=pl.ANY)] * (2 * sum(counts))
            if not first:
                in_specs.append(acc_spec)
                operands.append(acc)
            if last:
                out_shape = jax.ShapeDtypeStruct((rows, cols), jnp.bfloat16)
                out_spec = pl.BlockSpec((rows, width), lambda g, *_: (0, g))
            else:
                out_shape = jax.ShapeDtypeStruct((2, rows, cols), jnp.float32)
                out_spec = acc_spec
            return pl.pallas_call(
                functools.partial(block_kernel, row_tiles, col_tiles, chunk_tiles, counts, first, last),
                out_shape=out_shape,
                grid_spec=pltpu.PrefetchScalarGridSpec(
                    num_scalar_prefetch=2,
                    grid=(cols // width,),
                    in_specs=in_specs,
                    out_specs=out_spec,
                    scratch_shapes=[pltpu.VMEM((len(todo), 2, slots, TILE, TILE), jnp.bfloat16),
                                    pltpu.VMEM((len(todo), 2, depth, width), jnp.bfloat16),
                                    pltpu.SemaphoreType.DMA((2 * sum(counts),))],
                ),
                input_output_aliases={} if first or last else {len(operands) - 1: 0},
                compiler_params=pltpu.CompilerParams(vmem_limit_bytes=VMEM_LIMIT),
                cost_estimate=pl.CostEstimate(
                    flops=rows * depth, bytes_accessed=rows * depth, transcendentals=0),
                name="block",
            )(*operands)

        def along(value, s):
            return send(value, lambda rr, cc: ((rr + 4 * s) % R, cc))

        def with_sibling(value):
            return (value, send(value, sibling))

        paired = send(give, z_pair)
        far = [along(keep, s) for s in range(1, NZ // 2)]
        tok_mine = jnp.where(home, tokens, tok_other)
        tok_sib = send(jnp.where(home, tok_other, tokens), sibling)
        wide = tokens.shape[1]
        both = jnp.where(core == 0, jnp.concatenate([tok_mine, tok_sib], 1),
                         jnp.concatenate([tok_sib, tok_mine], 1))
        y = lax.axis_index("col") // 2
        tok_parts = [send(both, lambda rr, cc, s=s: (rr, (cc + 2 * s) % C)) for s in range(1, C // 2)]
        keep_x = send(keep, x_pair)
        (tok_parts, keep_x), (far, paired) = after((tok_parts, keep_x), (far, paired))
        tok = jnp.zeros((rows, wide * C), tokens.dtype)
        tok = lax.dynamic_update_slice_in_dim(tok, both, y * 2 * wide, 1)
        for s, part in enumerate(tok_parts, 1):
            source = (y - s) % (C // 2)
            tok = lax.dynamic_update_slice_in_dim(tok, part, source * 2 * wide, 1)
        half = 2 * slots // 3
        acc = add_blocks(None, [([with_sibling(keep)], r), ([with_sibling(keep_x)], r ^ 1)])
        far_paired = [along(paired, s) for s in range(1, NZ // 2)]
        far_x = [send(value, x_pair) for value in far]
        paired_x = send(paired, x_pair)
        todo = [([with_sibling(paired)], r ^ 2)]
        for s, value in enumerate(far, 1):
            todo.append(([with_sibling(value)], (r - 4 * s) % R))
        for n in range(0, len(todo), 2):
            acc = add_blocks(acc, todo[n:n + 2])
        far_paired, acc = after(far_paired, acc)
        (far_x, paired_x), far_paired = after((far_x, paired_x), far_paired)
        last_a = [send(value[:half], x_pair) for value in far_paired]
        last_b = [along(paired_x[half:], s) for s in range(1, NZ // 2)]
        todo = [([with_sibling(paired_x)], r ^ 3)]
        for s, value in enumerate(far_x, 1):
            todo.append(([with_sibling(value)], ((r - 4 * s) % R) ^ 1))
        for s, value in enumerate(far_paired, 1):
            todo.append(([with_sibling(value)], ((r ^ 2) - 4 * s) % R))
        for n in range(0, len(todo), 2):
            acc = add_blocks(acc, todo[n:n + 2])
        (last_a, last_b), acc = after((last_a, last_b), acc)
        for s in range(1, NZ // 2):
            acc = add_blocks(acc, [([with_sibling(last_a[s - 1]), with_sibling(last_b[s - 1])],
                                    (((r ^ 2) - 4 * s) % R) ^ 1)], last=s == NZ // 2 - 1)
        return send(acc, swap_out)

    placed = (P("row", "col"), P("row", "col"), P("row", "col"), P(None, "col"))
    return jax.shard_map(
        on_device, mesh=mesh, in_specs=placed, out_specs=P("row", "col"), check_vma=False
    )
```

profile of v0, /device:TPU:1, one launch (start us, length us, event | category | flops | bytes accessed | tf_op | source)
XLA Modules:
  0.0 414.2 jit_solution(4173825817639964889)
XLA Ops:
  0.0 0.7 constant_dynamic-slice_fusion
  0.7 0.6 reshape.26.mask_ref
  1.3 9.5 %pack.1 = (bf16[80,128,128]{2,1,0:T(8,128)(2,1)}, bf16[80,128,128]{2,1,0:T(8,128)(2,1)}) custom-call(s32[1]{0:T(128)} %bitcast.2.core_ref, s32[128]{0:T(128)} %reshape.26.mask_ref, bf16[512,4096]{1,0:T(8,128)(2,1)} %gate_ref.1, bf16[512,4096]{1,0:T(8,128)(2,1)} %up_ref.1), custom_call_target="tpu_custom_call" | custom-call | tf_op jit(solution)/shard_map/pack/pallas_call | solution.py:126
  10.8 0.0 collective-permute-start.1
  10.8 2.7 collective-permute-start.2
  13.4 23.8 %collective-permute-done.2 = bf16[512,1024]{1,0:T(8,128)(2,1)} collective-permute-done((bf16[512,1024]{1,0:T(8,128)(2,1)}, bf16[512,1024]{1,0:T(8,128)(2,1)}, u32[]{:S(2)}, u32[]{:S(2)}) %collective-permute-start.2) | collective-permute-done | bytes 1048608 | tf_op jit(solution)/shard_map/ppermute | solution.py:100
  37.3 0.0 collective-permute-done.1
  37.3 3.9 broadcast_select_fusion.2
  41.2 0.6 collective-permute-start.3
  41.8 3.9 broadcast_select_fusion
  45.7 1.3 collective-permute-start.5
  47.0 2.4 collective-permute-start.6
  49.5 1.4 collective-permute-start.7
  50.9 0.0 collective-permute-done.3
  50.9 2.5 broadcast_in_dim.3
  53.4 3.2 constant_dynamic-update-slice_fusion.1
  56.7 0.8 collective-permute-start.4
  57.5 1.1 collective-permute-start.13
  58.6 45.7 %collective-permute-done.5.rest_4_ = bf16[80,128,128]{2,1,0:T(8,128)(2,1)} collective-permute-done((bf16[80,128,128]{2,1,0:T(8,128)(2,1)S(1)}, bf16[80,128,128]{2,1,0:T(8,128)(2,1)}, u32[]{:S(2)}, u32[]{:S(2)}) %collective-permute-start.5) | collective-permute-done | bytes 2621472 | tf_op jit(solution)/shard_map/ppermute | solution.py:100
  104.3 58.3 %collective-permute-done.6.rest_4_ = bf16[80,128,128]{2,1,0:T(8,128)(2,1)} collective-permute-done((bf16[80,128,128]{2,1,0:T(8,128)(2,1)S(1)}, bf16[80,128,128]{2,1,0:T(8,128)(2,1)}, u32[]{:S(2)}, u32[]{:S(2)}) %collective-permute-start.6) | collective-permute-done | bytes 2621472 | tf_op jit(solution)/shard_map/ppermute | solution.py:100
  162.6 1.4 collective-permute-start.14
  164.0 0.1 collective-permute-start
  164.1 0.4 collective-permute-start.11
  164.5 0.1 collective-permute-start.12
  164.6 3.9 collective-permute-done
  168.4 1.1 collective-permute-start.10
  169.5 0.2 collective-permute-start.8
  169.7 1.3 copy-done.3
  171.0 0.8 collective-permute-done.14.rest_5_
  171.7 1.5 copy-done.4
  173.2 0.3 collective-permute-start.9
  173.5 0.6 add_add_fusion.1.info_ref
  174.1 0.1 mul.26
  174.2 0.1 eq.23
  174.3 0.2 multiply_reduce_fusion
  174.5 0.6 bitcast_select_fusion.codes_ref
  175.1 3.2 constant_dynamic-update-slice_fusion.rest_0_.rest_1_
  178.2 0.6 add_add_fusion.info_ref
  178.8 19.3 %block.5.rest_6_ = f32[2,512,4096]{2,1,0:T(8,128)} custom-call(s32[1024]{0:T(1024)} %bitcast_select_fusion.codes_ref, s32[3]{0:T(128)} %add_add_fusion.1.info_ref, bf16[512,4096]{1,0:T(8,128)(2,1)} %constant_dynamic-update-slice_fusion.rest_0_.rest_1_, bf16[512,4096]{1,0:T(8,128)(2,1)} %constant_dynamic-update-slice_fusion.rest_0_.rest_1_, ...), custom_call_target="tpu_custom_call" | custom-call | flops 262144 | bytes 262144 | tf_op jit(solution)/shard_map/block/pallas_call | solution.py:168
  198.1 23.0 %block.6.rest_6_ = f32[2,512,4096]{2,1,0:T(8,128)} custom-call(s32[1024]{0:T(1024)} %bitcast_select_fusion.codes_ref, s32[3]{0:T(128)} %add_add_fusion.info_ref, bf16[512,4096]{1,0:T(8,128)(2,1)} %constant_dynamic-update-slice_fusion.rest_0_.rest_1_, ...), custom_call_target="tpu_custom_call", output_to_operand_aliasing={{}: (8, {})} | custom-call | flops 262144 | bytes 262144 | tf_op jit(solution)/shard_map/block/pallas_call | solution.py:168
  221.1 63.0 %collective-permute-done.10.rest_1_ = bf16[80,128,128]{2,1,0:T(8,128)(2,1)} collective-permute-done((bf16[80,128,128]{2,1,0:T(8,128)(2,1)}, bf16[80,128,128]{2,1,0:T(8,128)(2,1)}, u32[]{:S(2)}, u32[]{:S(2)}) %collective-permute-start.10) | collective-permute-done | bytes 2621472 | tf_op jit(solution)/shard_map/ppermute | solution.py:100
  284.2 1.0 collective-permute-start.18
  285.2 0.1 collective-permute-start.19
  285.3 0.4 collective-permute-start.17
  285.7 2.9 slice.6
  288.6 0.2 collective-permute-start.15
  288.8 0.1 slice.7
  288.9 1.4 collective-permute-start.16
  290.3 0.7 pad_add_fusion.1.info_ref
  290.9 0.6 add_add_fusion.2.info_ref
  291.6 1.3 collective-permute-done.18.rest_3_
  292.9 1.0 collective-permute-done.19.rest_5_
  293.8 23.0 %block.7.rest_3_ = f32[2,512,4096]{2,1,0:T(8,128)} custom-call(s32[1024]{0:T(1024)} %bitcast_select_fusion.codes_ref, s32[3]{0:T(128)} %add_add_fusion.2.info_ref, bf16[512,4096]{1,0:T(8,128)(2,1)} %constant_dynamic-update-slice_fusion.rest_0_.rest_1_, ...), custom_call_target="tpu_custom_call", output_to_operand_aliasing={{}: (8, {})} | custom-call | flops 262144 | bytes 262144 | tf_op jit(solution)/shard_map/block/pallas_call | solution.py:168
  316.8 20.0 %block.8.rest_5_ = f32[2,512,4096]{2,1,0:T(8,128)} custom-call(s32[1024]{0:T(1024)} %bitcast_select_fusion.codes_ref, s32[2]{0:T(128)} %pad_add_fusion.1.info_ref, bf16[512,4096]{1,0:T(8,128)(2,1)} %constant_dynamic-update-slice_fusion.rest_0_.rest_1_, bf16[80,128,128]{2,1,0:T(8,128)(2,1)} %collective-permute-done.10.rest_1_, ...), custom_call_target="tpu_custom_call", output_to_operand_aliasing={{}: (5, {})} | custom-call | flops 262144 | bytes 262144 | tf_op jit(solution)/shard_map/block/pallas_call | solution.py:168
  336.8 0.4 collective-permute-start.20
  337.2 0.1 collective-permute-start.21
  337.4 0.6 pad_add_fusion.info_ref
  338.0 4.0 collective-permute-done.21.rest_4_
  342.0 0.9 copy-done.8
  342.9 1.2 copy-done.7
  344.2 17.3 %block.9 = bf16[512,4096]{1,0:T(8,128)(2,1)} custom-call(s32[1024]{0:T(1024)} %bitcast_select_fusion.codes_ref, s32[2]{0:T(128)} %pad_add_fusion.info_ref, bf16[512,4096]{1,0:T(8,128)(2,1)} %constant_dynamic-update-slice_fusion.rest_0_.rest_1_, bf16[53,128,128]{2,1,0:T(8,128)(2,1)} %collective-permute-done.15.rest_1_, ...), custom_call_target="tpu_custom_call" | custom-call | flops 262144 | bytes 262144 | tf_op jit(solution)/shard_map/block/pallas_call | solution.py:168
  361.5 4.3 %collective-permute-start.22 = (bf16[512,4096]{1,0:T(8,128)(2,1)}, bf16[512,4096]{1,0:T(8,128)(2,1)S(1)}, u32[]{:S(2)}, u32[]{:S(2)}) collective-permute-start(bf16[512,4096]{1,0:T(8,128)(2,1)} %block.9), channel_id=1, source_target_pairs={{0,0},{1,8},{2,2},{3,10},{4,4},{5,12},{6,6},{7,14},{8,1},{9,9},{10... | collective-permute-start | bytes 12582920 | tf_op jit(solution)/shard_map/ppermute | solution.py:100
  365.8 46.4 %collective-permute-done.22 = bf16[512,4096]{1,0:T(8,128)(2,1)S(1)} collective-permute-done((bf16[512,4096]{1,0:T(8,128)(2,1)}, bf16[512,4096]{1,0:T(8,128)(2,1)S(1)}, u32[]{:S(2)}, u32[]{:S(2)}) %collective-permute-start.22) | collective-permute-done | bytes 4194336 | tf_op jit(solution)/shard_map/ppermute | solution.py:100
  412.2 2.0 copy.14
  (29 shorter events, 0.1 us)
Async XLA Ops:
  10.8 26.5 %collective-permute-start.1 = (bf16[80,128,128]{2,1,0:T(8,128)(2,1)}, bf16[80,128,128]{2,1,0:T(8,128)(2,1)S(1)}, u32[]{:S(2)}, u32[]{:S(2)}) collective-permute-start(bf16[80,128,128]{2,1,0:T(8,128)(2,1)} %get-tuple-element.21), channel_id=1, source_target_pairs={{0,1},{1,0},{2,3},{3,2},{4,5},{5,4},{6,7},{7,6},{8,9},{9,8},{10,11... | collective-permute-start | bytes 7864328 | tf_op jit(solution)/shard_map/ppermute | solution.py:100
  10.8 26.5 %collective-permute-start.2 = (bf16[512,1024]{1,0:T(8,128)(2,1)}, bf16[512,1024]{1,0:T(8,128)(2,1)}, u32[]{:S(2)}, u32[]{:S(2)}) collective-permute-start(bf16[512,1024]{1,0:T(8,128)(2,1)} %param.4), channel_id=1, source_target_pairs={{0,8},{1,9},{2,10},{3,11},{4,12},{5,13},{6,14},{7,15},{8,0},{9,1},... | collective-permute-start | bytes 3145736 | tf_op jit(solution)/shard_map/ppermute | solution.py:100
  13.4 28.4 %copy-start.5 = (bf16[80,128,128]{2,1,0:T(8,128)(2,1)S(1)}, bf16[80,128,128]{2,1,0:T(8,128)(2,1)}, u32[]{:S(2)}) copy-start(bf16[80,128,128]{2,1,0:T(8,128)(2,1)} %get-tuple-element.23) | copy-start | bytes 7864324
  37.3 4.5 %copy-start.6 = (bf16[80,128,128]{2,1,0:T(8,128)(2,1)}, bf16[80,128,128]{2,1,0:T(8,128)(2,1)S(1)}, u32[]{:S(2)}) copy-start(bf16[80,128,128]{2,1,0:T(8,128)(2,1)S(1)} %collective-permute-done.1) | copy-start | bytes 7864324
  41.2 9.7 %collective-permute-start.3 = (bf16[512,1024]{1,0:T(8,128)(2,1)}, bf16[512,1024]{1,0:T(8,128)(2,1)}, u32[]{:S(2)}, u32[]{:S(2)}) collective-permute-start(bf16[512,1024]{1,0:T(8,128)(2,1)} %get-tuple-element.43), channel_id=1, source_target_pairs={{0,1},{1,0},{2,3},{3,2},{4,5},{5,4},{6,7},{7,6},{8,9},{9,8},{10,11... | collective-permute-start | bytes 3145736 | tf_op jit(solution)/shard_map/ppermute | solution.py:100
  45.7 11.8 %copy-start = (bf16[80,128,128]{2,1,0:T(8,128)(2,1)}, bf16[80,128,128]{2,1,0:T(8,128)(2,1)S(1)}, u32[]{:S(2)}) copy-start(bf16[80,128,128]{2,1,0:T(8,128)(2,1)S(1)} %get-tuple-element.42.rest_2_) | copy-start | bytes 7864324
  45.7 58.6 %collective-permute-start.5 = (bf16[80,128,128]{2,1,0:T(8,128)(2,1)S(1)}, bf16[80,128,128]{2,1,0:T(8,128)(2,1)}, u32[]{:S(2)}, u32[]{:S(2)}) collective-permute-start(bf16[80,128,128]{2,1,0:T(8,128)(2,1)S(1)} %get-tuple-element.42.rest_2_), channel_id=1, source_target_pairs={{0,4},{1,5},{2,6},{3,7},{4,0},{5,1},{6,2},{7,3},{8,12},{9,13},{10,... | collective-permute-start | bytes 7864328 | tf_op jit(solution)/shard_map/ppermute | solution.py:100
  47.0 115.5 %collective-permute-start.6 = (bf16[80,128,128]{2,1,0:T(8,128)(2,1)S(1)}, bf16[80,128,128]{2,1,0:T(8,128)(2,1)}, u32[]{:S(2)}, u32[]{:S(2)}) collective-permute-start(bf16[80,128,128]{2,1,0:T(8,128)(2,1)S(1)} %get-tuple-element.42.rest_2_), channel_id=1, source_target_pairs={{0,16},{1,17},{2,18},{3,19},{4,20},{5,21},{6,22},{7,23},{8,24},{9,... | collective-permute-start | bytes 7864328 | tf_op jit(solution)/shard_map/ppermute | solution.py:100
  49.5 113.1 %collective-permute-start.7 = (bf16[80,128,128]{2,1,0:T(8,128)(2,1)}, bf16[80,128,128]{2,1,0:T(8,128)(2,1)}, u32[]{:S(2)}, u32[]{:S(2)}) collective-permute-start(bf16[80,128,128]{2,1,0:T(8,128)(2,1)} %get-tuple-element.41), channel_id=1, source_target_pairs={{0,8},{1,9},{2,10},{3,11},{4,12},{5,13},{6,14},{7,15},{8,0},{9,1},... | collective-permute-start | bytes 7864328 | tf_op jit(solution)/shard_map/ppermute | solution.py:100
  50.9 2.5 copy-start.2
  53.4 110.5 %copy-start.9 = (s32[32,32]{1,0:T(8,128)S(1)}, s32[32,32]{1,0:T(8,128)}, u32[]{:S(2)}) copy-start(s32[32,32]{1,0:T(8,128)} %param.7) | copy-start | bytes 12292
  56.7 105.9 %collective-permute-start.4 = (bf16[512,2048]{1,0:T(8,128)(2,1)S(1)}, bf16[512,2048]{1,0:T(8,128)(2,1)}, u32[]{:S(2)}, u32[]{:S(2)}) collective-permute-start(bf16[512,2048]{1,0:T(8,128)(2,1)S(1)} %get-tuple-element.38), channel_id=1, source_target_pairs={{0,2},{1,3},{2,0},{3,1},{4,6},{5,7},{6,4},{7,5},{8,10},{9,11},{10,... | collective-permute-start | bytes 6291464 | tf_op jit(solution)/shard_map/ppermute | solution.py:100
  57.5 112.0 %collective-permute-start.13 = (bf16[80,128,128]{2,1,0:T(8,128)(2,1)S(1)}, bf16[80,128,128]{2,1,0:T(8,128)(2,1)S(1)}, u32[]{:S(2)}, u32[]{:S(2)}) collective-permute-start(bf16[80,128,128]{2,1,0:T(8,128)(2,1)S(1)} %get-tuple-element.42.rest_2_), channel_id=1, source_target_pairs={{0,1},{1,0},{2,3},{3,2},{4,5},{5,4},{6,7},{7,6},{8,9},{9,8},{10,11... | collective-permute-start | bytes 7864328 | tf_op jit(solution)/shard_map/ppermute | solution.py:100
  162.6 9.2 %collective-permute-start.14 = (bf16[80,128,128]{2,1,0:T(8,128)(2,1)}, bf16[80,128,128]{2,1,0:T(8,128)(2,1)S(1)}, u32[]{:S(2)}, u32[]{:S(2)}) collective-permute-start(bf16[80,128,128]{2,1,0:T(8,128)(2,1)} %collective-permute-done.5.rest_4_), channel_id=1, source_target_pairs={{0,1},{1,0},{2,3},{3,2},{4,5},{5,4},{6,7},{7,6},{8,9},{9,8},{10,11... | collective-permute-start | bytes 7864328 | tf_op jit(solution)/shard_map/ppermute | solution.py:100
  164.0 4.4 %collective-permute-start = (s32[32,32]{1,0:T(8,128)S(1)}, s32[32,32]{1,0:T(8,128)S(1)}, u32[]{:S(2)}, u32[]{:S(2)}) collective-permute-start(s32[32,32]{1,0:T(8,128)S(1)} %copy-done.9), channel_id=1, source_target_pairs={{0,1},{1,0},{2,3},{3,2},{4,5},{5,4},{6,7},{7,6},{8,9},{9,8},{10,11... | collective-permute-start | bytes 12296 | tf_op jit(solution)/shard_map/ppermute | solution.py:100
  164.1 34.0 %collective-permute-start.11 = (bf16[80,128,128]{2,1,0:T(8,128)(2,1)}, bf16[80,128,128]{2,1,0:T(8,128)(2,1)}, u32[]{:S(2)}, u32[]{:S(2)}) collective-permute-start(bf16[80,128,128]{2,1,0:T(8,128)(2,1)} %collective-permute-done.7.rest_2_), channel_id=1, source_target_pairs={{0,1},{1,0},{2,3},{3,2},{4,5},{5,4},{6,7},{7,6},{8,9},{9,8},{10,11... | collective-permute-start | bytes 7864328 | tf_op jit(solution)/shard_map/ppermute | solution.py:100
  164.5 33.6 %collective-permute-start.12 = (bf16[80,128,128]{2,1,0:T(8,128)(2,1)}, bf16[80,128,128]{2,1,0:T(8,128)(2,1)}, u32[]{:S(2)}, u32[]{:S(2)}) collective-permute-start(bf16[80,128,128]{2,1,0:T(8,128)(2,1)} %collective-permute-done.6.rest_4_), channel_id=1, source_target_pairs={{0,1},{1,0},{2,3},{3,2},{4,5},{5,4},{6,7},{7,6},{8,9},{9,8},{10,11... | collective-permute-start | bytes 7864328 | tf_op jit(solution)/shard_map/ppermute | solution.py:100
  168.4 115.7 %collective-permute-start.10 = (bf16[80,128,128]{2,1,0:T(8,128)(2,1)}, bf16[80,128,128]{2,1,0:T(8,128)(2,1)}, u32[]{:S(2)}, u32[]{:S(2)}) collective-permute-start(bf16[80,128,128]{2,1,0:T(8,128)(2,1)} %collective-permute-done.7.rest_2_), channel_id=1, source_target_pairs={{0,16},{1,17},{2,18},{3,19},{4,20},{5,21},{6,22},{7,23},{8,24},{9,... | collective-permute-start | bytes 7864328 | tf_op jit(solution)/shard_map/ppermute | solution.py:100
  169.5 1.5 copy-start.3
  169.5 114.6 %collective-permute-start.8 = (bf16[80,128,128]{2,1,0:T(8,128)(2,1)}, bf16[80,128,128]{2,1,0:T(8,128)(2,1)}, u32[]{:S(2)}, u32[]{:S(2)}) collective-permute-start(bf16[80,128,128]{2,1,0:T(8,128)(2,1)} %collective-permute-done.6.rest_4_), channel_id=1, source_target_pairs={{0,4},{1,5},{2,6},{3,7},{4,0},{5,1},{6,2},{7,3},{8,12},{9,13},{10,... | collective-permute-start | bytes 7864328 | tf_op jit(solution)/shard_map/ppermute | solution.py:100
  171.7 1.5 copy-start.4
  173.2 110.9 %collective-permute-start.9 = (bf16[80,128,128]{2,1,0:T(8,128)(2,1)}, bf16[80,128,128]{2,1,0:T(8,128)(2,1)S(1)}, u32[]{:S(2)}, u32[]{:S(2)}) collective-permute-start(bf16[80,128,128]{2,1,0:T(8,128)(2,1)} %collective-permute-done.7.rest_2_), channel_id=1, source_target_pairs={{0,4},{1,5},{2,6},{3,7},{4,0},{5,1},{6,2},{7,3},{8,12},{9,13},{10,... | collective-permute-start | bytes 7864328 | tf_op jit(solution)/shard_map/ppermute | solution.py:100
  284.2 4.8 %copy-start.1 = (bf16[80,128,128]{2,1,0:T(8,128)(2,1)}, bf16[80,128,128]{2,1,0:T(8,128)(2,1)S(1)}, u32[]{:S(2)}) copy-start(bf16[80,128,128]{2,1,0:T(8,128)(2,1)S(1)} %collective-permute-done.9.rest_2_) | copy-start | bytes 7864324
  284.2 8.7 %collective-permute-start.18 = (bf16[80,128,128]{2,1,0:T(8,128)(2,1)S(1)}, bf16[80,128,128]{2,1,0:T(8,128)(2,1)}, u32[]{:S(2)}, u32[]{:S(2)}) collective-permute-start(bf16[80,128,128]{2,1,0:T(8,128)(2,1)S(1)} %collective-permute-done.9.rest_2_), channel_id=1, source_target_pairs={{0,1},{1,0},{2,3},{3,2},{4,5},{5,4},{6,7},{7,6},{8,9},{9,8},{10,11... | collective-permute-start | bytes 7864328 | tf_op jit(solution)/shard_map/ppermute | solution.py:100
  285.2 8.6 %collective-permute-start.19 = (bf16[80,128,128]{2,1,0:T(8,128)(2,1)}, bf16[80,128,128]{2,1,0:T(8,128)(2,1)}, u32[]{:S(2)}, u32[]{:S(2)}) collective-permute-start(bf16[80,128,128]{2,1,0:T(8,128)(2,1)} %collective-permute-done.8.rest_4_), channel_id=1, source_target_pairs={{0,1},{1,0},{2,3},{3,2},{4,5},{5,4},{6,7},{7,6},{8,9},{9,8},{10,11... | collective-permute-start | bytes 7864328 | tf_op jit(solution)/shard_map/ppermute | solution.py:100
  285.3 31.5 %collective-permute-start.17 = (bf16[80,128,128]{2,1,0:T(8,128)(2,1)}, bf16[80,128,128]{2,1,0:T(8,128)(2,1)}, u32[]{:S(2)}, u32[]{:S(2)}) collective-permute-start(bf16[80,128,128]{2,1,0:T(8,128)(2,1)} %collective-permute-done.10.rest_1_), channel_id=1, source_target_pairs={{0,1},{1,0},{2,3},{3,2},{4,5},{5,4},{6,7},{7,6},{8,9},{9,8},{10,11... | collective-permute-start | bytes 7864328 | tf_op jit(solution)/shard_map/ppermute | solution.py:100
  288.6 48.2 %collective-permute-start.15 = (bf16[53,128,128]{2,1,0:T(8,128)(2,1)}, bf16[53,128,128]{2,1,0:T(8,128)(2,1)}, u32[]{:S(2)}, u32[]{:S(2)}) collective-permute-start(bf16[53,128,128]{2,1,0:T(8,128)(2,1)} %slice.6), channel_id=1, source_target_pairs={{0,4},{1,5},{2,6},{3,7},{4,0},{5,1},{6,2},{7,3},{8,12},{9,13},{10,... | collective-permute-start | bytes 5210120 | tf_op jit(solution)/shard_map/ppermute | solution.py:100
  288.9 47.8 %collective-permute-start.16 = (bf16[27,128,128]{2,1,0:T(8,128)(2,1)S(1)}, bf16[27,128,128]{2,1,0:T(8,128)(2,1)}, u32[]{:S(2)}, u32[]{:S(2)}) collective-permute-start(bf16[27,128,128]{2,1,0:T(8,128)(2,1)S(1)} %slice.7), channel_id=1, source_target_pairs={{0,16},{1,17},{2,18},{3,19},{4,20},{5,21},{6,22},{7,23},{8,24},{9,... | collective-permute-start | bytes 2654216 | tf_op jit(solution)/shard_map/ppermute | solution.py:100
  336.8 5.2 %collective-permute-start.20 = (bf16[53,128,128]{2,1,0:T(8,128)(2,1)}, bf16[53,128,128]{2,1,0:T(8,128)(2,1)S(1)}, u32[]{:S(2)}, u32[]{:S(2)}) collective-permute-start(bf16[53,128,128]{2,1,0:T(8,128)(2,1)} %collective-permute-done.15.rest_1_), channel_id=1, source_target_pairs={{0,1},{1,0},{2,3},{3,2},{4,5},{5,4},{6,7},{7,6},{8,9},{9,8},{10,11... | collective-permute-start | bytes 5210120 | tf_op jit(solution)/shard_map/ppermute | solution.py:100
  337.2 4.7 %collective-permute-start.21 = (bf16[27,128,128]{2,1,0:T(8,128)(2,1)}, bf16[27,128,128]{2,1,0:T(8,128)(2,1)S(1)}, u32[]{:S(2)}, u32[]{:S(2)}) collective-permute-start(bf16[27,128,128]{2,1,0:T(8,128)(2,1)} %collective-permute-done.16.rest_2_), channel_id=1, source_target_pairs={{0,1},{1,0},{2,3},{3,2},{4,5},{5,4},{6,7},{7,6},{8,9},{9,8},{10,11... | collective-permute-start | bytes 2654216 | tf_op jit(solution)/shard_map/ppermute | solution.py:100
  342.0 1.0 copy-start.8
  342.9 1.2 copy-start.7
  361.5 50.7 %collective-permute-start.22 = (bf16[512,4096]{1,0:T(8,128)(2,1)}, bf16[512,4096]{1,0:T(8,128)(2,1)S(1)}, u32[]{:S(2)}, u32[]{:S(2)}) collective-permute-start(bf16[512,4096]{1,0:T(8,128)(2,1)} %block.9), channel_id=1, source_target_pairs={{0,0},{1,8},{2,2},{3,10},{4,4},{5,12},{6,6},{7,14},{8,1},{9,9},{10... | collective-permute-start | bytes 12582920 | tf_op jit(solution)/shard_map/ppermute | solution.py:100
where the time goes:
time: 415 us; the launch traced here: 414 us
  waiting for transfers between devices  248 us (60%)
  Pallas kernels  112 us (27%)
  starting transfers between devices  21.8 us (5%)
  local copies, waits for them, and re-layouts  17.1 us (4%)
  other arithmetic  15 us (4%)
    ppermute x23, waiting for transfers between devices, send(): return lax.ppermute(value, axes, pairs)  248 us
    pallas_call x5, Pallas kernels, add_blocks(): pl.pallas_call(functools.partial(block_kernel, row_tiles, col_tiles, chun...  103 us
    ppermute x23, starting transfers between devices, send(): return lax.ppermute(value, axes, pairs)  21.8 us
    pallas_call x1, Pallas kernels, on_device(): pl.pallas_call(functools.partial(pack_kernel, row_tiles, col_tiles), out_...  9.52 us
  transfers between devices with their start and end apart: 23, of which 10 were waited for; matrix products, arithmetic and copies ran while one was open for 5% of the time, Pallas kernels for 21%

commit v1 on v0

v1 whole, which is shorter than its diff:
```python
import functools

import jax
import jax.numpy as jnp
from jax import lax
from jax.experimental import pallas as pl
from jax.experimental.pallas import tpu as pltpu
from jax.sharding import PartitionSpec as P

TILE = 128
VMEM_LIMIT = 60 * 1024 * 1024
MESH = pl.DeviceIdType.MESH


def pack_kernel(row_tiles, col_tiles, core_ref, mask_ref, gate_ref, up_ref, mine_ref, other_ref):
    core = core_ref[0]

    def column(j, slot):
        cols = pl.ds(pl.multiple_of(j * TILE, TILE), TILE)
        for i in range(row_tiles):
            kept = mask_ref[i * col_tiles + j]
            rows = pl.ds(i * TILE, TILE)

            @pl.when((kept == 1) & (core == 0))
            def _(slot=slot):
                mine_ref[slot] = gate_ref[rows, cols]
                other_ref[slot] = up_ref[rows, cols]

            @pl.when((kept == 1) & (core == 1))
            def _(slot=slot):
                mine_ref[slot] = up_ref[rows, cols]
                other_ref[slot] = gate_ref[rows, cols]

            slot = slot + kept
        return slot

    lax.fori_loop(0, col_tiles, column, jnp.int32(0))


def split(total, parts):
    parts = min(parts, total)
    edges = [total * n // parts for n in range(parts + 1)]
    return [(a, b - a) for a, b in zip(edges, edges[1:])]


def main_kernel(R, C, row_tiles, col_tiles, slots, codes_ref, tok_in, mine_ref, other_ref, out_ref, *scratch):
    NZ, NY = R // 2, C // 2
    rows, wide = tok_in.shape
    depth = row_tiles * TILE
    first = row_tiles * col_tiles // 2
    chunk_tiles = min(4, col_tiles // 4)
    width = chunk_tiles * TILE
    per_core = col_tiles // (4 * chunk_tiles)
    parts = [(0, *v) for v in split(first, 4)] + [(1, *v) for v in split(slots - first, 2)]
    nc = len(parts)
    firsts = [n for n in range(nc) if parts[n][0] == 0]
    lasts = [n for n in range(nc) if parts[n][0] == 1]

    scratch = list(scratch)
    take = lambda n: [scratch.pop(0) for _ in range(n)]
    own = take(2)
    far = [None] + [take(2) for _ in range(1, NZ)]
    across = [take(2) for _ in range(NZ)]
    tok, acc, dense, given, done = take(5)
    (w_send, w_recv, w_here, z_send, z_recv, x_send, x_recv, t_here, t_send, t_recv, ts_send, ts_recv,
     a_send, a_recv, o_send, os_send, o_recv, free) = take(18)

    r, c = lax.axis_index("row"), lax.axis_index("col")
    core = c % 2
    parity = (r // 2) % 2
    sibling = (r, c ^ 1)
    x_pair = (r ^ 1, c)
    owner = (c // 2) * 2 + parity

    def remote(src, dst, send, recv, device):
        return pltpu.make_async_remote_copy(
            src_ref=src, dst_ref=dst, send_sem=send, recv_sem=recv, device_id=device, device_id_type=MESH)

    partners = [sibling, x_pair, (r ^ 2, c ^ 1)]
    partners += [(r ^ (2 * d), c) for d in range(1, NZ)]
    partners += [(r, (c + 2 * s) % C) for s in range(1, NY)]
    barrier = pltpu.get_barrier_semaphore()
    for device in partners:
        pl.semaphore_signal(barrier, inc=1, device_id=device, device_id_type=MESH)
    pl.semaphore_wait(barrier, len(partners))

    def own_part(index, n):
        half, start, size = parts[n]
        return own[half].at[index, pl.ds(start, size)]

    def packed_part(ref, n):
        return ref.at[pl.ds(parts[n][1] + (first if parts[n][0] else 0), parts[n][2])]

    def piece_part(piece, n):
        half, start, size = parts[n]
        return piece[half].at[pl.ds(start, size)]

    def w_copy(n):
        return remote(packed_part(other_ref, n), own_part(core, n), w_send.at[n], w_recv.at[n], sibling)

    def w_arrival(n):
        return remote(packed_part(other_ref, n), own_part(1 - core, n), w_send.at[n], w_recv.at[n], sibling)

    def w_local(n):
        return pltpu.make_async_copy(packed_part(mine_ref, n), own_part(core, n), w_here.at[n])

    def z_copy(d, n):
        index = parity if d % 2 == 0 else 1 - parity
        return remote(own_part(index, n), piece_part(far[d], n), z_send.at[d, n], z_recv.at[d, n],
                      (r ^ (2 * d), c))

    def x_copy(d, n):
        src = own_part(parity, n) if d == 0 else piece_part(far[d], n)
        return remote(src, piece_part(across[d], n), x_send.at[d, n], x_recv.at[d, n], x_pair)

    def tok_place(group, col):
        return tok.at[pl.ds(group * rows, rows), pl.ds(pl.multiple_of(col * wide, TILE), wide)]

    def tok_copy(group, s):
        src = tok_in if group == 0 else tok_place(1, c)
        if s == 0:
            return remote(tok_in, tok_place(1, c), t_send.at[1, 0], t_recv.at[1, 0], (r ^ 2, c))
        return remote(src, tok_place(group, c), t_send.at[group, s], t_recv.at[group, s], (r, (c + 2 * s) % C))

    def tok_arrival(group, s):
        return remote(tok_in, tok_place(group, (c - 2 * s) % C), t_send.at[group, s], t_recv.at[group, s],
                      sibling)

    def tok_share(group, s):
        col = (c - 2 * s) % C
        src = tok_in if group == 0 and s == 0 else tok_place(group, col)
        return remote(src, tok_place(group, col), ts_send.at[group, s], ts_recv.at[group, s], sibling)

    def tok_shared(group, s):
        return remote(tok_in, tok_place(group, ((c ^ 1) - 2 * s) % C), ts_send.at[group, s],
                      ts_recv.at[group, s], sibling)

    tok_local = pltpu.make_async_copy(tok_in, tok_place(0, c), t_here)

    w_copy(0).start()
    w_local(0).start()
    tok_copy(1, 0).start()
    for n in range(1, nc):
        w_copy(n).start()
        w_local(n).start()
    for s in range(1, NY):
        tok_copy(0, s).start()
    cut = [d for d in range(2, NZ, 2)] + [d for d in range(3, NZ, 2)]
    order = [(d, n) for d in cut for n in firsts] + [(d, n) for d in cut for n in lasts]
    ahead = 2
    for n in range(nc):
        w_arrival(n).wait_recv()
        w_local(n).wait()
        if n < ahead:
            z_copy(1, n).start()
            z_copy(*order[n]).start()
        if n in firsts:
            x_copy(0, n).start()
    tok_share(0, 0).start()
    tok_local.start()

    def clear(n, carry):
        acc[n] = jnp.zeros(acc.shape[1:], acc.dtype)
        return carry

    lax.fori_loop(0, acc.shape[0], clear, 0)

    def job(piece, index, source, half, bounds):
        count, place = bounds

        def step(n, carry):
            chunk = half * 2 * per_core + place(n)
            for j in range(chunk_tiles):
                for i in range(row_tiles):
                    code = codes_ref[(source * row_tiles + i) * col_tiles + chunk * chunk_tiles + j]
                    low = jnp.minimum(jnp.maximum(code, 0), first - 1)
                    tile = piece[0][low] if index is None else piece[0][index, low]
                    zero = jnp.zeros_like(tile)
                    value = jnp.where(code >= 0, tile, zero)
                    if half:
                        high = jnp.maximum(code - first, 0)
                        late = piece[1][high] if index is None else piece[1][index, high]
                        value = jnp.where(code >= first, late, value)
                    dense[pl.ds(i * TILE, TILE), pl.ds(j * TILE, TILE)] = value
            lhs = tok[:, pl.ds(pl.multiple_of(source * depth, TILE), depth)]
            acc[chunk] += jnp.dot(lhs, dense[...], preferred_element_type=jnp.float32)
            return carry

        lax.fori_loop(0, count, step, 0)

    every = (2 * per_core, lambda n: n)
    theirs = (per_core, lambda n: (1 - core) * per_core + n)
    ours = (per_core, lambda n: core * per_core + n)

    def near_job(d, half, bounds=every):
        if d == 0:
            job(own, parity, r, half, bounds)
        else:
            job(far[d], None, r ^ (2 * d), half, bounds)

    arrived = set()

    def across_wait(d, ns):
        for n in ns:
            if (d, n) not in arrived:
                arrived.add((d, n))
                x_copy(d, n).wait_recv()

    def across_job(d, half, bounds=every):
        across_wait(d, firsts if half == 0 else range(nc))
        job(across[d], None, r ^ (2 * d) ^ 1, half, bounds)

    def sums_copy(half, i):
        chunk = half * 2 * per_core + (1 - core) * per_core + i
        return remote(acc.at[chunk], given.at[i], a_send.at[half, i], a_recv.at[half, i], sibling)

    def out_place(chunk):
        return out_ref.at[:, pl.ds(pl.multiple_of(chunk * width, TILE), width)]

    def done_part(half, i, group):
        return done.at[half * per_core + i, pl.ds(group * rows, rows)]

    def out_copy(half, i):
        chunk = half * 2 * per_core + core * per_core + i
        return remote(done_part(half, i, 1), out_place(chunk), o_send.at[half, i], o_recv.at[chunk], (r ^ 2, owner))

    def out_share(half, i):
        chunk = half * 2 * per_core + core * per_core + i
        return remote(done_part(half, i, 0), out_place(chunk), os_send.at[half, i], o_recv.at[chunk], sibling)

    def out_local(half, i):
        chunk = half * 2 * per_core + core * per_core + i
        return pltpu.make_async_copy(done_part(half, i, 0), out_place(chunk), o_recv.at[chunk])

    def finish(half, i):
        sums_copy(half, i).wait_recv()
        chunk = half * 2 * per_core + core * per_core + i
        block = min(128, rows)

        def rows_step(n, carry):
            here = pl.ds(pl.multiple_of(n * block, block), block)
            a, b = acc[chunk, here], given[i, here]
            gate = jnp.where(core == 0, a, b)
            up = jnp.where(core == 0, b, a)
            done[half * per_core + i, here] = (gate / (1.0 + jnp.exp(-gate)) * up).astype(done.dtype)
            return carry

        lax.fori_loop(rows // block, 2 * rows // block, rows_step, 0)
        out_copy(half, i).start()
        lax.fori_loop(0, rows // block, rows_step, 0)

        @pl.when(core == parity)
        def _():
            out_local(half, i).start()

        @pl.when(core != parity)
        def _():
            out_share(half, i).start()

    tok_arrival(1, 0).wait_recv()
    for s in range(1, NY):
        tok_copy(1, s).start()
    tok_share(1, 0).start()
    for s in range(1, NY):
        tok_arrival(0, s).wait_recv()
        tok_share(0, s).start()

    pair_order = firsts + lasts
    state = dict(pair=0)

    def pass_on(s):
        d, n = order[s]
        z_copy(d, n).wait_recv()
        x_copy(d, n).start()
        if s + ahead < len(order):
            z_copy(*order[s + ahead]).start()

    def pair_step():
        m = state["pair"]
        if m < nc:
            n = pair_order[m]
            z_copy(1, n).wait_recv()
            if n in firsts:
                x_copy(1, n).start()
            if m + ahead < nc:
                z_copy(1, pair_order[m + ahead]).start()
            state["pair"] = m + 1

    near_first = [("near", 0, 0), ("near", 0, 1), ("across", 0, 0)]
    ready = []
    head = len(firsts)
    total_first = len(cut) * head
    for s in range(total_first):
        pass_on(s)
        pair_step()
        if s == 0:
            for q in range(1, NY):
                tok_arrival(1, q).wait_recv()
                tok_share(1, q).start()
        if s == 1 or total_first == 1:
            tok_local.wait()
            for g in range(2):
                for q in range(NY):
                    tok_shared(g, q).wait_recv()
            ready += near_first
        if s + 1 == head:
            while state["pair"] < nc:
                pair_step()
            ready += [("near", 1, 0), ("near", 1, 1), ("across", 1, 0)]
        if (s + 1) % head == 0:
            ready += [("near", cut[s // head], 0)]
            if s // head:
                ready += [("across", cut[s // head - 1], 0)]
        if s + 3 == total_first:
            for n in lasts:
                x_copy(0, n).start()
                x_copy(1, n).start()
        budget = 2 if s + 1 < total_first else len(ready)
        while ready and budget:
            kind, d, half = ready.pop(0)
            (near_job if kind == "near" else across_job)(d, half)
            budget -= 1

    last = cut[-1]
    across_job(last, 0, theirs)
    for i in range(per_core):
        sums_copy(0, i).start()
    across_job(last, 0, ours)
    late = [("across", 0), ("across", 1)]
    for m in range(len(cut) * len(lasts)):
        pass_on(total_first + m)
        if m == 0:
            for i in range(per_core):
                finish(0, i)
                sums_copy(0, i).wait_send()
            pl.semaphore_signal(free, inc=1, device_id=sibling, device_id_type=MESH)
        e = m // len(lasts)
        if (m + 1) % len(lasts) == 0 and e + 1 < len(cut):
            late += [("near", cut[e])]
        if m % len(lasts) == 0 and e:
            late += [("across", cut[e - 1])]
        if m + 1 < len(cut) * len(lasts):
            for _ in range(min(2, len(late))):
                kind, d = late.pop(0)
                (near_job if kind == "near" else across_job)(d, 1)
    for kind, d in late:
        (near_job if kind == "near" else across_job)(d, 1)
    near_job(last, 1)
    across_job(last, 1, theirs)
    pl.semaphore_wait(free, 1)
    for i in range(per_core):
        sums_copy(1, i).start()
    across_job(last, 1, ours)
    for i in range(per_core):
        finish(1, i)

    for n in range(nc):
        w_copy(n).wait_send()
        for d in range(NZ):
            x_copy(d, n).wait_send()
            if d:
                z_copy(d, n).wait_send()
    for g in range(2):
        for s in range(NY):
            if g or s:
                tok_copy(g, s).wait_send()
            tok_share(g, s).wait_send()
    for i in range(per_core):
        sums_copy(1, i).wait_send()
        for half in range(2):
            out_copy(half, i).wait_send()

            @pl.when(core != parity)
            def _(half=half, i=i):
                out_share(half, i).wait_send()

    for chunk in range(4 * per_core):
        pltpu.make_async_copy(done_part(0, 0, 0), out_place(chunk), o_recv.at[chunk]).wait()


def solution(mesh):
    R, C = mesh.shape["row"], mesh.shape["col"]
    NZ, NY = R // 2, C // 2
    axes = ("row", "col")

    def on_device(tokens, gate_weight, up_weight, tile_mask):
        depth, cols = gate_weight.shape
        row_tiles, col_tiles = depth // TILE, cols // TILE
        tiles = row_tiles * col_tiles
        slots = 5 * tiles // 8
        rows = tokens.shape[0]
        r = lax.axis_index("row")
        core = lax.axis_index("col") % 2
        home = ((r // 2) % 2) == core

        mask_sib = lax.ppermute(tile_mask, axes, [(d, d ^ 1) for d in range(R * C)])
        smem = pl.BlockSpec(memory_space=pltpu.SMEM)
        vmem = pl.BlockSpec(memory_space=pltpu.VMEM)
        hbm = pl.BlockSpec(memory_space=pl.ANY)
        own_mask = lax.dynamic_slice_in_dim(tile_mask, r * row_tiles, row_tiles, 0).reshape(-1)
        piece = jax.ShapeDtypeStruct((slots, TILE, TILE), gate_weight.dtype)
        mine, other = pl.pallas_call(
            functools.partial(pack_kernel, row_tiles, col_tiles),
            out_shape=(piece, piece),
            in_specs=[smem, smem, vmem, vmem],
            out_specs=(vmem, vmem),
            compiler_params=pltpu.CompilerParams(vmem_limit_bytes=VMEM_LIMIT),
            name="pack",
        )(core.reshape(1).astype(jnp.int32), own_mask, gate_weight, up_weight)

        job_mask = jnp.where(home, tile_mask, mask_sib).reshape(R, row_tiles, col_tiles)
        place = jnp.arange(tiles)
        place = (place % col_tiles) * row_tiles + place // col_tiles
        upto = (place[None, :] <= place[:, None]).astype(jnp.int32)
        job_mask = job_mask.reshape(R, tiles)
        slot = jnp.sum(job_mask[:, None, :] * upto[None], axis=2) - 1
        codes = jnp.where(job_mask == 1, slot, -1).reshape(-1)

        first = tiles // 2
        chunk_tiles = min(4, col_tiles // 4)
        width = chunk_tiles * TILE
        per_core = col_tiles // (4 * chunk_tiles)
        nc = len(split(first, 4)) + len(split(slots - first, 2))
        bf16, f32 = jnp.bfloat16, jnp.float32
        pieces = [pltpu.VMEM((2, first, TILE, TILE), bf16), pltpu.VMEM((2, slots - first, TILE, TILE), bf16)]
        for _ in range(2 * NZ - 1):
            pieces += [pltpu.VMEM((first, TILE, TILE), bf16), pltpu.VMEM((slots - first, TILE, TILE), bf16)]
        sem = pltpu.SemaphoreType.DMA
        return pl.pallas_call(
            functools.partial(main_kernel, R, C, row_tiles, col_tiles, slots),
            out_shape=jax.ShapeDtypeStruct((rows, cols), bf16),
            in_specs=[smem, hbm, hbm, hbm],
            out_specs=hbm,
            scratch_shapes=pieces + [
                pltpu.VMEM((2 * rows, tokens.shape[1] * C), bf16),
                pltpu.VMEM((4 * per_core, 2 * rows, width), f32),
                pltpu.VMEM((depth, width), bf16),
                pltpu.VMEM((per_core, 2 * rows, width), f32),
                pltpu.VMEM((2 * per_core, 2 * rows, width), bf16),
                sem((nc,)), sem((nc,)), sem((nc,)),
                sem((NZ, nc)), sem((NZ, nc)), sem((NZ, nc)), sem((NZ, nc)),
                sem, sem((2, NY)), sem((2, NY)), sem((2, NY)), sem((2, NY)),
                sem((2, per_core)), sem((2, per_core)), sem((2, per_core)), sem((2, per_core)),
                sem((4 * per_core,)), pltpu.SemaphoreType.REGULAR,
            ],
            compiler_params=pltpu.CompilerParams(
                vmem_limit_bytes=VMEM_LIMIT, collective_id=0, has_side_effects=True),
            cost_estimate=pl.CostEstimate(
                flops=8 * rows * depth * R * cols // 2, bytes_accessed=rows * cols * 2, transcendentals=rows * cols),
            name="main",
        )(codes, tokens, mine, other)

    placed = (P("row", "col"), P("row", "col"), P("row", "col"), P(None, "col"))
    return jax.shard_map(
        on_device, mesh=mesh, in_specs=placed, out_specs=P("row", "col"), check_vma=False
    )
```

time: 415 us -> 319 us (0.77)
  waiting for transfers between devices: 248 us -> 0.01 us
  Pallas kernels: 112 us -> 311 us
  starting transfers between devices: 21.8 us -> 0.06 us
  other arithmetic: 15 us -> 0.91 us
  local copies, waits for them, and re-layouts: 17.1 us -> 6.22 us
    ppermute x23 -> x1, waiting for transfers between devices: 248 us -> 0.01 us  [on_device(): mask_sib = lax.ppermute(tile_mask, axes, [(d, d ^ 1) for d in range(R * C)])]
    pallas_call x5 -> x1, Pallas kernels: 103 us -> 302 us  [on_device(): pl.pallas_call(functools.partial(main_kernel, R, C, row_tiles, col_tiles,...]
    ppermute x23 -> x1, starting transfers between devices: 21.8 us -> 0.06 us  [on_device(): mask_sib = lax.ppermute(tile_mask, axes, [(d, d ^ 1) for d in range(R * C)])]
    select_n x2 -> x0, other arithmetic: 7.85 us -> none  [the longest x1 3.95 us: on_device(): tok_sib = send(jnp.where(home, tok_other, tokens), sibling)]
  transfers between devices with their start and end apart: 23 -> 1, of which waited for: 10 -> 0; matrix products, arithmetic and copies ran while one was open for 5% -> 0% of each run, Pallas kernels for 21% -> 3%
where the time goes in v1:
time: 319 us; the launch traced here: 318 us
  Pallas kernels  311 us (97%)
  local copies, waits for them, and re-layouts  6.22 us (2%)
    pallas_call x1, Pallas kernels, on_device(): pl.pallas_call(functools.partial(main_kernel, R, C, row_tiles, col_tiles,...  302 us
    pallas_call x1, Pallas kernels, on_device(): pl.pallas_call(functools.partial(pack_kernel, row_tiles, col_tiles), out_...  8.72 us
  transfers between devices with their start and end apart: 1, of which 0 were waited for; matrix products, arithmetic and copies ran while one was open for 0% of the time, Pallas kernels for 3%

profile of v1, /device:TPU:1, one launch (start us, length us, event | category | flops | bytes accessed | tf_op | source)
XLA Modules:
  0.0 317.8 jit_solution(3831119545784296132)
XLA Ops:
  0.0 0.1 collective-permute-start
  0.1 0.1 compare_convert_fusion
  0.2 0.7 constant_dynamic-slice_fusion
  0.9 0.7 reshape.87.mask_ref
  1.5 0.0 copy-start
  1.5 8.7 %pack.1 = (bf16[80,128,128]{2,1,0:T(8,128)(2,1)}, bf16[80,128,128]{2,1,0:T(8,128)(2,1)}) custom-call(s32[1]{0:T(128)} %bitcast.1.core_ref, s32[128]{0:T(128)} %reshape.87.mask_ref, bf16[512,4096]{1,0:T(8,128)(2,1)} %gate_ref.1, bf16[512,4096]{1,0:T(8,128)(2,1)} %up_ref.1), custom_call_target="tpu_custom_call" | custom-call | tf_op jit(solution)/shard_map/pack/pallas_call | solution.py:402
  10.2 0.0 collective-permute-done
  10.2 0.0 copy-done
  10.3 0.1 eq.17
  10.3 0.1 mul.32
  10.4 0.2 multiply_reduce_fusion
  10.6 0.6 bitcast_select_fusion.codes_ref
  11.2 301.9 %main.1 = bf16[512,4096]{1,0:T(8,128)(2,1)} custom-call(s32[1024]{0:T(1024)} %bitcast_select_fusion.codes_ref, bf16[512,1024]{1,0:T(8,128)(2,1)} %tok_in.1, bf16[80,128,128]{2,1,0:T(8,128)(2,1)} %get-tuple-element.7.mine_ref, bf16[80,128,128]{2,1,0:T(8,128)(2,1)} %get-tuple-element.8.other_ref), custom_call_target="tpu_custom_call" | custom-call | flops 34359738368 | bytes 4194304 | tf_op jit(solution)/shard_map/main/pallas_call | solution.py:429
  313.1 4.7 %copy.6 = bf16[512,4096]{1,0:T(8,128)(2,1)} copy(bf16[512,4096]{1,0:T(8,128)(2,1)} %main.1) | data formatting | bytes 8388608
  (2 shorter events, 0.0 us)
Async XLA Ops:
  0.0 10.2 %collective-permute-start = (s32[32,32]{1,0:T(8,128)}, s32[32,32]{1,0:T(8,128)S(1)}, u32[]{:S(2)}, u32[]{:S(2)}) collective-permute-start(s32[32,32]{1,0:T(8,128)} %param.7), channel_id=1, source_target_pairs={{0,1},{1,0},{2,3},{3,2},{4,5},{5,4},{6,7},{7,6},{8,9},{9,8},{10,11... | collective-permute-start | bytes 12296 | tf_op jit(solution)/shard_map/ppermute | solution.py:396
  1.5 8.7 %copy-start = (s32[32,32]{1,0:T(8,128)S(1)}, s32[32,32]{1,0:T(8,128)}, u32[]{:S(2)}) copy-start(s32[32,32]{1,0:T(8,128)} %param.7) | copy-start | bytes 12292

commit v2 on v1

v2 whole, which is shorter than its diff:
```python
import functools

import jax
import jax.numpy as jnp
from jax import lax
from jax.experimental import pallas as pl
from jax.experimental.pallas import tpu as pltpu
from jax.sharding import PartitionSpec as P

TILE = 128
VMEM_LIMIT = 60 * 1024 * 1024
FA, LB, AHEAD, BUDGET, LATE = 8, 4, 4, 1, 2
T1, T2, T3 = 0.5, 0.75, 1.0
MESH = pl.DeviceIdType.MESH


def copy_kernel(in_ref, out_ref):
    out_ref[...] = in_ref[...]


def split(total, parts):
    parts = min(parts, total)
    edges = [total * n // parts for n in range(parts + 1)]
    return [(a, b - a) for a, b in zip(edges, edges[1:])]


def main_kernel(R, C, row_tiles, col_tiles, slots, codes_ref, order_ref, tok_in, gate_in, up_in, out_ref, *scratch):
    NZ, NY = R // 2, C // 2
    rows, wide = tok_in.shape
    depth = row_tiles * TILE
    first = row_tiles * col_tiles // 2
    chunk_tiles = min(4, col_tiles // 4)
    width = chunk_tiles * TILE
    per_core = col_tiles // (4 * chunk_tiles)
    parts = [(0, *v) for v in split(first, FA)] + [(1, *v) for v in split(slots - first, LB)]
    nc = len(parts)
    firsts = [n for n in range(nc) if parts[n][0] == 0]
    lasts = [n for n in range(nc) if parts[n][0] == 1]

    scratch = list(scratch)
    take = lambda n: [scratch.pop(0) for _ in range(n)]
    own = take(2)
    other = take(2)
    far = [None] + [take(2) for _ in range(1, NZ)]
    across = [take(2) for _ in range(NZ)]
    tok, acc, dense, given, done = take(5)
    (w_send, w_recv, w_load, z_send, z_recv, x_send, x_recv, t_here, t_send, t_recv, ts_send, ts_recv,
     a_send, a_recv, o_send, os_send, o_recv, free) = take(18)

    r, c = lax.axis_index("row"), lax.axis_index("col")
    core = c % 2
    parity = (r // 2) % 2
    sibling = (r, c ^ 1)
    x_pair = (r ^ 1, c)
    owner = (c // 2) * 2 + parity

    def remote(src, dst, send, recv, device):
        return pltpu.make_async_remote_copy(
            src_ref=src, dst_ref=dst, send_sem=send, recv_sem=recv, device_id=device, device_id_type=MESH)

    loads = [pltpu.make_async_copy(ref, tok.at[pl.ds(n * depth, depth), pl.ds(0, col_tiles * TILE)], w_load.at[n])
             for n, ref in enumerate((gate_in, up_in))]
    for load in loads:
        load.start()
    for load in loads:
        load.wait()

    def pack(half, start, s):
        i, j = order_ref[r * slots + start + s], order_ref[(R + r) * slots + start + s]
        cols = pl.ds(j * TILE, TILE)
        mine_row = (core * row_tiles + i) * TILE
        other_row = ((1 - core) * row_tiles + i) * TILE
        own[half][core, s] = tok[pl.ds(mine_row, TILE), cols]
        other[half][s] = tok[pl.ds(other_row, TILE), cols]

    for half, start, stop in ((0, 0, first), (1, first, slots)):
        def pack_step(s, carry, half=half, start=start):
            pack(half, start, s)
            return carry

        lax.fori_loop(0, stop - start, pack_step, 0, unroll=min(4, stop - start))

    partners = [sibling, x_pair, (r ^ 2, c ^ 1)]
    partners += [(r ^ (2 * d), c) for d in range(1, NZ)]
    partners += [(r, (c + 2 * s) % C) for s in range(1, NY)]
    barrier = pltpu.get_barrier_semaphore()
    for device in partners:
        pl.semaphore_signal(barrier, inc=1, device_id=device, device_id_type=MESH)
    pl.semaphore_wait(barrier, len(partners))

    def own_part(index, n):
        half, start, size = parts[n]
        return own[half].at[index, pl.ds(start, size)]

    def piece_part(piece, n):
        half, start, size = parts[n]
        return piece[half].at[pl.ds(start, size)]

    def w_copy(n):
        return remote(piece_part(other, n), own_part(core, n), w_send.at[n], w_recv.at[n], sibling)

    def w_arrival(n):
        return remote(piece_part(other, n), own_part(1 - core, n), w_send.at[n], w_recv.at[n], sibling)

    def z_copy(d, n):
        index = parity if d % 2 == 0 else 1 - parity
        return remote(own_part(index, n), piece_part(far[d], n), z_send.at[d, n], z_recv.at[d, n],
                      (r ^ (2 * d), c))

    def x_copy(d, n):
        src = own_part(parity, n) if d == 0 else piece_part(far[d], n)
        return remote(src, piece_part(across[d], n), x_send.at[d, n], x_recv.at[d, n], x_pair)

    def tok_place(group, col):
        return tok.at[pl.ds(group * rows, rows), pl.ds(pl.multiple_of(col * wide, TILE), wide)]

    def tok_copy(group, s):
        src = tok_in if group == 0 else tok_place(1, c)
        if s == 0:
            return remote(tok_in, tok_place(1, c), t_send.at[1, 0], t_recv.at[1, 0], (r ^ 2, c))
        return remote(src, tok_place(group, c), t_send.at[group, s], t_recv.at[group, s], (r, (c + 2 * s) % C))

    def tok_arrival(group, s):
        return remote(tok_in, tok_place(group, (c - 2 * s) % C), t_send.at[group, s], t_recv.at[group, s],
                      sibling)

    def tok_share(group, s):
        col = (c - 2 * s) % C
        src = tok_in if group == 0 and s == 0 else tok_place(group, col)
        return remote(src, tok_place(group, col), ts_send.at[group, s], ts_recv.at[group, s], sibling)

    def tok_shared(group, s):
        return remote(tok_in, tok_place(group, ((c ^ 1) - 2 * s) % C), ts_send.at[group, s],
                      ts_recv.at[group, s], sibling)

    tok_local = pltpu.make_async_copy(tok_in, tok_place(0, c), t_here)

    w_copy(0).start()
    tok_copy(1, 0).start()
    for n in range(1, nc):
        w_copy(n).start()
    for s in range(1, NY):
        tok_copy(0, s).start()
    cut = [d for d in range(2, NZ, 2)] + [d for d in range(3, NZ, 2)]
    order = [(d, n) for d in cut for n in firsts] + [(d, n) for d in cut for n in lasts]
    ahead = AHEAD
    for n in range(nc):
        w_arrival(n).wait_recv()
        if n < ahead:
            z_copy(1, n).start()
            z_copy(*order[n]).start()
        x_copy(0, n).start()
    tok_share(0, 0).start()
    tok_local.start()

    def clear(n, carry):
        acc[n] = jnp.zeros(acc.shape[1:], acc.dtype)
        return carry

    lax.fori_loop(0, acc.shape[0], clear, 0)

    def job(piece, index, source, half, bounds):
        count, place, after = bounds

        def step(n, carry):
            chunk = half * 2 * per_core + place(n)
            for j in range(chunk_tiles):
                for i in range(row_tiles):
                    code = codes_ref[(source * row_tiles + i) * col_tiles + chunk * chunk_tiles + j]
                    low = jnp.minimum(jnp.maximum(code, 0), first - 1)
                    tile = piece[0][low] if index is None else piece[0][index, low]
                    zero = jnp.zeros_like(tile)
                    value = jnp.where(code >= 0, tile, zero)
                    if half:
                        high = jnp.maximum(code - first, 0)
                        late = piece[1][high] if index is None else piece[1][index, high]
                        value = jnp.where(code >= first, late, value)
                    dense[pl.ds(i * TILE, TILE), pl.ds(j * TILE, TILE)] = value
            lhs = tok[:, pl.ds(pl.multiple_of(source * depth, TILE), depth)]
            acc[chunk] += jnp.dot(lhs, dense[...], preferred_element_type=jnp.float32)
            if after:
                after(n)
            return carry

        lax.fori_loop(0, count, step, 0)

    def sums_copy(half, i, group):
        chunk = half * 2 * per_core + (1 - core) * per_core + i
        part = pl.ds(group * rows, rows)
        return remote(acc.at[chunk, part], given.at[i, part], a_send.at[half, i, group],
                      a_recv.at[half, i, group], sibling)

    every = (2 * per_core, lambda n: n, None)
    theirs = [(per_core, lambda n: (1 - core) * per_core + n, lambda n, h=h: sums_copy(h, n, 1).start())
              for h in range(2)]
    ours = (per_core, lambda n: core * per_core + n, None)

    def near_job(d, half, bounds=every):
        if d == 0:
            job(own, parity, r, half, bounds)
        else:
            job(far[d], None, r ^ (2 * d), half, bounds)

    arrived = set()

    def across_wait(d, ns):
        for n in ns:
            if (d, n) not in arrived:
                arrived.add((d, n))
                x_copy(d, n).wait_recv()

    def across_job(d, half, bounds=every):
        across_wait(d, firsts if half == 0 else range(nc))
        job(across[d], None, r ^ (2 * d) ^ 1, half, bounds)

    def out_place(chunk):
        return out_ref.at[:, pl.ds(pl.multiple_of(chunk * width, TILE), width)]

    def done_part(half, i, group):
        return done.at[half * per_core + i, pl.ds(group * rows, rows)]

    def out_copy(half, i):
        chunk = half * 2 * per_core + core * per_core + i
        return remote(done_part(half, i, 1), out_place(chunk), o_send.at[half, i], o_recv.at[chunk], (r ^ 2, owner))

    def out_share(half, i):
        chunk = half * 2 * per_core + core * per_core + i
        return remote(done_part(half, i, 0), out_place(chunk), os_send.at[half, i], o_recv.at[chunk], sibling)

    def out_local(half, i):
        chunk = half * 2 * per_core + core * per_core + i
        return pltpu.make_async_copy(done_part(half, i, 0), out_place(chunk), o_recv.at[chunk])

    def finish(half, i, group):
        sums_copy(half, i, group).wait_recv()
        chunk = half * 2 * per_core + core * per_core + i
        block = min(128, rows)

        def rows_step(n, carry):
            here = pl.ds(pl.multiple_of(group * rows + n * block, block), block)
            a, b = acc[chunk, here], given[i, here]
            gate = jnp.where(core == 0, a, b)
            up = jnp.where(core == 0, b, a)
            done[half * per_core + i, here] = (gate / (1.0 + jnp.exp(-gate)) * up).astype(done.dtype)
            return carry

        lax.fori_loop(0, rows // block, rows_step, 0)
        if group:
            out_copy(half, i).start()
        else:
            @pl.when(core == parity)
            def _():
                out_local(half, i).start()

            @pl.when(core != parity)
            def _():
                out_share(half, i).start()

    pair_order = firsts + lasts
    state = dict(pair=0)

    def pass_on(s):
        d, n = order[s]
        z_copy(d, n).wait_recv()
        x_copy(d, n).start()
        if s + ahead < len(order):
            z_copy(*order[s + ahead]).start()

    def pair_step():
        m = state["pair"]
        if m < nc:
            n = pair_order[m]
            z_copy(1, n).wait_recv()
            x_copy(1, n).start()
            if m + ahead < nc:
                z_copy(1, pair_order[m + ahead]).start()
            state["pair"] = m + 1

    def tokens_1():
        tok_arrival(1, 0).wait_recv()
        for s in range(1, NY):
            tok_copy(1, s).start()
        tok_share(1, 0).start()
        for s in range(1, NY):
            tok_arrival(0, s).wait_recv()
            tok_share(0, s).start()

    def tokens_2():
        for q in range(1, NY):
            tok_arrival(1, q).wait_recv()
            tok_share(1, q).start()

    def tokens_3():
        tok_local.wait()
        for g in range(2):
            for q in range(NY):
                tok_shared(g, q).wait_recv()

    head = len(firsts)
    total_first = len(cut) * head
    plan = {}

    def at(position, item):
        plan.setdefault(min(max(int(position * head) - 1, 0), total_first - 1), []).append(item)

    at(T1, tokens_1)
    at(T2, tokens_2)
    at(T3, tokens_3)
    for item in [("near", 0, 0), ("near", 0, 1), ("across", 0, 0), ("across", 0, 1), ("near", 1, 0)]:
        at(T3, item)
    for n, d in enumerate(cut):
        at(n + 1, ("near", d, 0))
        if n:
            at(n + 1, ("across", cut[n - 1], 0))
    at(1.5, ("across", 1, 0))
    at(1.5, ("near", 1, 1))
    ready = []
    for s in range(total_first):
        pass_on(s)
        pair_step()
        for item in plan.get(s, []):
            if callable(item):
                item()
            else:
                ready.append(item)
        if s + 1 == total_first:
            while state["pair"] < nc:
                pair_step()
        budget = BUDGET if s + 1 < total_first else len(ready)
        while ready and budget:
            kind, d, half = ready[0]
            if (kind, d, half) == ("near", 1, 1) and state["pair"] < nc:
                break
            ready.pop(0)
            (near_job if kind == "near" else across_job)(d, half)
            budget -= 1

    last = cut[-1]
    across_job(last, 0, theirs[0])
    across_job(last, 0, ours)
    for i in range(per_core):
        sums_copy(0, i, 0).start()
    late = [functools.partial(finish, 0, i, group) for group in (1, 0) for i in range(per_core)]

    def release():
        for group in range(2):
            for i in range(per_core):
                sums_copy(0, i, group).wait_send()
        pl.semaphore_signal(free, inc=1, device_id=sibling, device_id_type=MESH)

    late += [release, functools.partial(across_job, 1, 1)]
    steps = len(cut) * len(lasts)
    for m in range(steps):
        pass_on(total_first + m)
        e = m // len(lasts)
        if (m + 1) % len(lasts) == 0 and e + 1 < len(cut):
            late += [functools.partial(near_job, cut[e], 1)]
        if m % len(lasts) == 0 and e:
            late += [functools.partial(across_job, cut[e - 1], 1)]
        if m + 1 < steps:
            for _ in range(min(LATE, len(late))):
                late.pop(0)()
    for item in late:
        item()
    near_job(last, 1)
    pl.semaphore_wait(free, 1)
    across_job(last, 1, theirs[1])
    across_job(last, 1, ours)
    for i in range(per_core):
        sums_copy(1, i, 0).start()
    for group in (1, 0):
        for i in range(per_core):
            finish(1, i, group)

    for n in range(nc):
        w_copy(n).wait_send()
        for d in range(NZ):
            x_copy(d, n).wait_send()
            if d:
                z_copy(d, n).wait_send()
    for g in range(2):
        for s in range(NY):
            if g or s:
                tok_copy(g, s).wait_send()
            tok_share(g, s).wait_send()
    for i in range(per_core):
        for group in range(2):
            sums_copy(1, i, group).wait_send()
        for half in range(2):
            out_copy(half, i).wait_send()

            @pl.when(core != parity)
            def _(half=half, i=i):
                out_share(half, i).wait_send()

    for chunk in range(4 * per_core):
        pltpu.make_async_copy(done_part(0, 0, 0), out_place(chunk), o_recv.at[chunk]).wait()


def solution(mesh):
    R, C = mesh.shape["row"], mesh.shape["col"]
    NZ, NY = R // 2, C // 2
    axes = ("row", "col")

    def on_device(tokens, gate_weight, up_weight, tile_mask):
        depth, cols = gate_weight.shape
        row_tiles, col_tiles = depth // TILE, cols // TILE
        tiles = row_tiles * col_tiles
        slots = 5 * tiles // 8
        rows = tokens.shape[0]
        r = lax.axis_index("row")
        core = lax.axis_index("col") % 2
        home = ((r // 2) % 2) == core

        mask_sib = lax.ppermute(tile_mask, axes, [(d, d ^ 1) for d in range(R * C)])
        smem = pl.BlockSpec(memory_space=pltpu.SMEM)
        hbm = pl.BlockSpec(memory_space=pl.ANY)
        place = jnp.arange(tiles)
        place = (place % col_tiles) * row_tiles + place // col_tiles
        upto = (place[None, :] <= place[:, None]).astype(jnp.int32)

        def slot_codes(mask):
            mask = mask.reshape(R, tiles)
            return jnp.where(mask == 1, jnp.sum(mask[:, None, :] * upto[None], axis=2) - 1, -1)

        here = slot_codes(tile_mask)
        match = here[:, None, :] == jnp.arange(slots)[None, :, None]
        corner = jnp.stack([jnp.arange(tiles) // col_tiles, jnp.arange(tiles) % col_tiles])
        order = jnp.sum(jnp.where(match[None], corner[:, None, None, :], 0), axis=3).reshape(-1)
        codes = slot_codes(jnp.where(home, tile_mask, mask_sib)).reshape(-1)

        first = tiles // 2
        chunk_tiles = min(4, col_tiles // 4)
        width = chunk_tiles * TILE
        per_core = col_tiles // (4 * chunk_tiles)
        nc = len(split(first, FA)) + len(split(slots - first, LB))
        bf16, f32 = jnp.bfloat16, jnp.float32
        pieces = [pltpu.VMEM((2, first, TILE, TILE), bf16), pltpu.VMEM((2, slots - first, TILE, TILE), bf16)]
        for _ in range(2 * NZ):
            pieces += [pltpu.VMEM((first, TILE, TILE), bf16), pltpu.VMEM((slots - first, TILE, TILE), bf16)]
        sem = pltpu.SemaphoreType.DMA
        hidden = pl.pallas_call(
            functools.partial(main_kernel, R, C, row_tiles, col_tiles, slots),
            out_shape=jax.ShapeDtypeStruct((rows, cols), bf16),
            in_specs=[smem, smem, hbm, hbm, hbm],
            out_specs=hbm,
            scratch_shapes=pieces + [
                pltpu.VMEM((2 * rows, tokens.shape[1] * C), bf16),
                pltpu.VMEM((4 * per_core, 2 * rows, width), f32),
                pltpu.VMEM((depth, width), bf16),
                pltpu.VMEM((per_core, 2 * rows, width), f32),
                pltpu.VMEM((2 * per_core, 2 * rows, width), bf16),
                sem((nc,)), sem((nc,)), sem((2,)),
                sem((NZ, nc)), sem((NZ, nc)), sem((NZ, nc)), sem((NZ, nc)),
                sem, sem((2, NY)), sem((2, NY)), sem((2, NY)), sem((2, NY)),
                sem((2, per_core, 2)), sem((2, per_core, 2)), sem((2, per_core)), sem((2, per_core)),
                sem((4 * per_core,)), pltpu.SemaphoreType.REGULAR,
            ],
            compiler_params=pltpu.CompilerParams(
                vmem_limit_bytes=VMEM_LIMIT, collective_id=0, has_side_effects=True),
            cost_estimate=pl.CostEstimate(
                flops=8 * rows * depth * R * cols // 2, bytes_accessed=rows * cols * 2, transcendentals=rows * cols),
            name="main",
        )(codes, order, tokens, gate_weight, up_weight)
        part = pl.BlockSpec((rows // 4, cols), lambda n: (n, 0))
        return pl.pallas_call(
            copy_kernel,
            out_shape=jax.ShapeDtypeStruct((rows, cols), bf16),
            grid=(4,),
            in_specs=[part],
            out_specs=part,
            name="place",
        )(hidden)

    placed = (P("row", "col"), P("row", "col"), P("row", "col"), P(None, "col"))
    return jax.shard_map(
        on_device, mesh=mesh, in_specs=placed, out_specs=P("row", "col"), check_vma=False
    )
```

time: 319 us -> 303 us (0.950)
  Pallas kernels: 311 us -> 297 us
  local copies, waits for them, and re-layouts: 6.22 us -> 1.63 us
    pallas_call x1, Pallas kernels: 302 us -> 292 us  [on_device(): pl.pallas_call(functools.partial(main_kernel, R, C, row_tiles, col_tiles,...]
    unnamed x3 -> x0, local copies, waits for them, and re-layouts: 4.7 us -> none
    pallas_call x1, Pallas kernels: 8.72 us -> 4.74 us  [on_device(): pl.pallas_call(copy_kernel, out_shape=jax.ShapeDtypeStruct((rows, cols),...]
  transfers between devices with their start and end apart: 1 -> 1, of which waited for: 0 -> 1; matrix products, arithmetic and copies ran while one was open for 0% -> 0% of each run, Pallas kernels for 3% -> 0%
where the time goes in v2:
time: 303 us; the launch traced here: 301 us
  Pallas kernels  297 us (98%)
    pallas_call x1, Pallas kernels, on_device(): pl.pallas_call(functools.partial(main_kernel, R, C, row_tiles, col_tiles,...  292 us
  transfers between devices with their start and end apart: 1, of which 1 were waited for; matrix products, arithmetic and copies ran while one was open for 0% of the time, Pallas kernels for 0%

profile of v2, /device:TPU:1, one launch (start us, length us, event | category | flops | bytes accessed | tf_op | source)
XLA Modules:
  0.0 300.6 jit_solution(9929935769323788433)
XLA Ops:
  0.0 0.1 collective-permute-start
  0.1 0.1 compare_convert_fusion
  0.2 0.8 reshape.133
  1.0 0.4 collective-permute-done
  1.4 0.1 eq.42
  1.5 0.1 mul.44
  1.6 0.3 multiply_reduce_fusion
  1.9 0.1 iota_compare_fusion
  2.0 0.3 select_reduce_fusion
  2.3 0.7 reshape.134.order_ref
  3.0 0.6 bitcast_select_fusion.codes_ref
  3.6 292.3 %main.1.in_ref = bf16[512,4096]{1,0:T(8,128)(2,1)} custom-call(s32[1024]{0:T(1024)} %bitcast_select_fusion.codes_ref, s32[1280]{0:T(1024)} %reshape.134.order_ref, bf16[512,1024]{1,0:T(8,128)(2,1)} %tok_in.1, bf16[512,4096]{1,0:T(8,128)(2,1)} %gate_in.1, bf16[512,4096]{1,0:T(8,128)(2,1)} %up_in.1), custom_call_target="tpu_custom_call" | custom-call | flops 34359738368 | bytes 4194304 | tf_op jit(solution)/shard_map/main/pallas_call | solution.py:442
  295.9 4.7 %place.1 = bf16[512,4096]{1,0:T(8,128)(2,1)} custom-call(bf16[512,4096]{1,0:T(8,128)(2,1)} %main.1.in_ref), custom_call_target="tpu_custom_call" | custom-call | tf_op jit(solution)/shard_map/place/pallas_call | solution.py:466
  (5 shorter events, 0.0 us)
Async XLA Ops:
  0.0 1.4 collective-permute-start

commit v3 on v2

v3 whole, which is shorter than its diff:
```python
import functools

import jax
import jax.numpy as jnp
from jax import lax
from jax.experimental import pallas as pl
from jax.experimental.pallas import tpu as pltpu
from jax.sharding import PartitionSpec as P

TILE = 128
VMEM_LIMIT = 63 * 1024 * 1024
AHEAD, LAG = 4, 3
T1, T2, T3 = 0.5, 0.75, 1.0
MESH = pl.DeviceIdType.MESH


def copy_kernel(in_ref, out_ref):
    out_ref[...] = in_ref[...]


def split(total, parts):
    parts = min(parts, total)
    edges = [total * n // parts for n in range(parts + 1)]
    return [(a, b - a) for a, b in zip(edges, edges[1:])]


def levels_of(row_tiles, col_tiles, slots):
    cuts = [col_tiles // 4, col_tiles // 2] if col_tiles >= 8 else [col_tiles // 2]
    return [(row_tiles * cols, cols) for cols in cuts] + [(slots, col_tiles)]


def parts_of(levels):
    parts, start = [], 0
    for n, (stop, _) in enumerate(levels):
        parts += [(n, *v) for v in split(stop - start, 4)]
        start = stop
    return parts


def main_kernel(R, C, row_tiles, col_tiles, slots, codes_ref, order_ref, tok_in, gate_in, up_in, out_ref, *scratch):
    NZ, NY = R // 2, C // 2
    rows, wide = tok_in.shape
    depth = row_tiles * TILE
    levels = levels_of(row_tiles, col_tiles, slots)
    L = len(levels)
    bottoms = [0] + [stop for stop, _ in levels[:-1]]
    chunk_tiles = min(4, levels[0][1] // 2)
    width = chunk_tiles * TILE
    lefts = [0] + [cols // chunk_tiles for _, cols in levels]
    per_core = [(b - a) // 2 for a, b in zip(lefts, lefts[1:])]
    parts = parts_of(levels)
    nc = len(parts)
    at_level = [[n for n in range(nc) if parts[n][0] == v] for v in range(L)]

    scratch = list(scratch)
    take = lambda n: [scratch.pop(0) for _ in range(n)]
    own = take(L)
    other = take(L)
    far = [None] + [take(L) for _ in range(1, NZ)]
    across = [take(L) for _ in range(NZ)]
    tok, acc, dense, given, done = take(5)
    (w_send, w_recv, w_load, z_send, z_recv, x_send, x_recv, t_here, t_send, t_recv, ts_send, ts_recv,
     a_send, a_recv, o_send, os_send, o_recv, free) = take(18)

    r, c = lax.axis_index("row"), lax.axis_index("col")
    core = c % 2
    parity = (r // 2) % 2
    sibling = (r, c ^ 1)
    x_pair = (r ^ 1, c)
    owner = (c // 2) * 2 + parity

    def remote(src, dst, send, recv, device):
        return pltpu.make_async_remote_copy(
            src_ref=src, dst_ref=dst, send_sem=send, recv_sem=recv, device_id=device, device_id_type=MESH)

    loads = [pltpu.make_async_copy(ref, tok.at[pl.ds(n * depth, depth), pl.ds(0, col_tiles * TILE)], w_load.at[n])
             for n, ref in enumerate((gate_in, up_in))]
    for load in loads:
        load.start()
    for load in loads:
        load.wait()

    for v in range(L):
        def pack_step(s, carry, v=v):
            n = r * slots + bottoms[v] + s
            i, j = order_ref[n], order_ref[R * slots + n]
            cols = pl.ds(j * TILE, TILE)
            mine_row = (core * row_tiles + i) * TILE
            other_row = ((1 - core) * row_tiles + i) * TILE
            own[v][core, s] = tok[pl.ds(mine_row, TILE), cols]
            other[v][s] = tok[pl.ds(other_row, TILE), cols]
            return carry

        count = levels[v][0] - bottoms[v]
        lax.fori_loop(0, count, pack_step, 0, unroll=min(4, count))

    partners = [sibling, x_pair, (r ^ 2, c ^ 1)]
    partners += [(r ^ (2 * d), c) for d in range(1, NZ)]
    partners += [(r, (c + 2 * s) % C) for s in range(1, NY)]
    barrier = pltpu.get_barrier_semaphore()
    for device in partners:
        pl.semaphore_signal(barrier, inc=1, device_id=device, device_id_type=MESH)
    pl.semaphore_wait(barrier, len(partners))

    def own_part(index, n):
        half, start, size = parts[n]
        return own[half].at[index, pl.ds(start, size)]

    def piece_part(piece, n):
        half, start, size = parts[n]
        return piece[half].at[pl.ds(start, size)]

    def w_copy(n):
        return remote(piece_part(other, n), own_part(core, n), w_send.at[n], w_recv.at[n], sibling)

    def w_arrival(n):
        return remote(piece_part(other, n), own_part(1 - core, n), w_send.at[n], w_recv.at[n], sibling)

    def z_copy(d, n):
        index = parity if d % 2 == 0 else 1 - parity
        return remote(own_part(index, n), piece_part(far[d], n), z_send.at[d, n], z_recv.at[d, n],
                      (r ^ (2 * d), c))

    def x_copy(d, n):
        src = own_part(parity, n) if d == 0 else piece_part(far[d], n)
        return remote(src, piece_part(across[d], n), x_send.at[d, n], x_recv.at[d, n], x_pair)

    def tok_place(group, col):
        return tok.at[pl.ds(group * rows, rows), pl.ds(pl.multiple_of(col * wide, TILE), wide)]

    def tok_copy(group, s):
        src = tok_in if group == 0 else tok_place(1, c)
        if s == 0:
            return remote(tok_in, tok_place(1, c), t_send.at[1, 0], t_recv.at[1, 0], (r ^ 2, c))
        return remote(src, tok_place(group, c), t_send.at[group, s], t_recv.at[group, s], (r, (c + 2 * s) % C))

    def tok_arrival(group, s):
        return remote(tok_in, tok_place(group, (c - 2 * s) % C), t_send.at[group, s], t_recv.at[group, s],
                      sibling)

    def tok_share(group, s):
        col = (c - 2 * s) % C
        src = tok_in if group == 0 and s == 0 else tok_place(group, col)
        return remote(src, tok_place(group, col), ts_send.at[group, s], ts_recv.at[group, s], sibling)

    def tok_shared(group, s):
        return remote(tok_in, tok_place(group, ((c ^ 1) - 2 * s) % C), ts_send.at[group, s],
                      ts_recv.at[group, s], sibling)

    tok_local = pltpu.make_async_copy(tok_in, tok_place(0, c), t_here)

    w_copy(0).start()
    tok_copy(1, 0).start()
    for n in range(1, nc):
        w_copy(n).start()
    for s in range(1, NY):
        tok_copy(0, s).start()
    cut = [d for d in range(2, NZ, 2)] + [d for d in range(3, NZ, 2)]
    order = [(d, n) for v in range(L) for d in cut for n in at_level[v]]
    ahead = AHEAD
    for n in range(nc):
        w_arrival(n).wait_recv()
        if n < ahead:
            z_copy(1, n).start()
            z_copy(*order[n]).start()
        x_copy(0, n).start()
    tok_share(0, 0).start()
    tok_local.start()

    def clear(n, carry):
        acc[n] = jnp.zeros(acc.shape[1:], acc.dtype)
        return carry

    lax.fori_loop(0, acc.shape[0], clear, 0)

    def job(piece, index, source, v, bounds):
        count, place, after = bounds

        def step(n, carry):
            chunk = place(n)
            for j in range(chunk_tiles):
                for i in range(row_tiles):
                    code = codes_ref[(source * row_tiles + i) * col_tiles + chunk * chunk_tiles + j]
                    value = None
                    for u in range(v + 1):
                        size = levels[u][0] - bottoms[u]
                        slot = jnp.minimum(jnp.maximum(code - bottoms[u], 0), size - 1)
                        tile = piece[u][slot] if index is None else piece[u][index, slot]
                        value = jnp.where(code >= bottoms[u], tile, jnp.zeros_like(tile) if value is None else value)
                    dense[pl.ds(i * TILE, TILE), pl.ds(j * TILE, TILE)] = value
            lhs = tok[:, pl.ds(pl.multiple_of(source * depth, TILE), depth)]
            acc[chunk] += jnp.dot(lhs, dense[...], preferred_element_type=jnp.float32)
            if after:
                after(n)
            return carry

        lax.fori_loop(0, count, step, 0)

    def our_chunk(v, i):
        return lefts[v] + core * per_core[v] + i

    def their_chunk(v, i):
        return lefts[v] + (1 - core) * per_core[v] + i

    def sums_copy(v, i, group):
        part = pl.ds(group * rows, rows)
        return remote(acc.at[their_chunk(v, i), part], given.at[i, part], a_send.at[v, i, group],
                      a_recv.at[v, i, group], sibling)

    every = [(2 * per_core[v], lambda n, v=v: lefts[v] + n, None) for v in range(L)]
    theirs = [(per_core[v], functools.partial(their_chunk, v), None) for v in range(L)]
    sent = [(per_core[v], functools.partial(their_chunk, v), lambda n, v=v: sums_copy(v, n, 1).start())
            for v in range(L)]
    ours = [(per_core[v], functools.partial(our_chunk, v), None) for v in range(L)]

    def near_job(d, v, bounds=every):
        if d == 0:
            job(own, parity, r, v, bounds[v])
        else:
            job(far[d], None, r ^ (2 * d), v, bounds[v])

    arrived = set()

    def across_job(d, v, bounds=every):
        for n in range(nc):
            if parts[n][0] <= v and (d, n) not in arrived:
                arrived.add((d, n))
                x_copy(d, n).wait_recv()
        job(across[d], None, r ^ (2 * d) ^ 1, v, bounds[v])

    def out_place(chunk):
        return out_ref.at[:, pl.ds(pl.multiple_of(chunk * width, TILE), width)]

    def done_part(v, i, group):
        return done.at[sum(per_core[:v]) + i, pl.ds(group * rows, rows)]

    def out_copy(v, i):
        return remote(done_part(v, i, 1), out_place(our_chunk(v, i)), o_send.at[sum(per_core[:v]) + i],
                      o_recv.at[our_chunk(v, i)], (r ^ 2, owner))

    def out_share(v, i):
        return remote(done_part(v, i, 0), out_place(our_chunk(v, i)), os_send.at[sum(per_core[:v]) + i],
                      o_recv.at[our_chunk(v, i)], sibling)

    def out_local(v, i):
        return pltpu.make_async_copy(done_part(v, i, 0), out_place(our_chunk(v, i)), o_recv.at[our_chunk(v, i)])

    def finish(v, i, group):
        sums_copy(v, i, group).wait_recv()
        chunk = our_chunk(v, i)
        block = min(128, rows)

        def rows_step(n, carry):
            here = pl.ds(pl.multiple_of(group * rows + n * block, block), block)
            a, b = acc[chunk, here], given[i, here]
            gate = jnp.where(core == 0, a, b)
            up = jnp.where(core == 0, b, a)
            done[sum(per_core[:v]) + i, here] = (gate / (1.0 + jnp.exp(-gate)) * up).astype(done.dtype)
            return carry

        lax.fori_loop(0, rows // block, rows_step, 0)
        if group:
            out_copy(v, i).start()
        else:
            @pl.when(core == parity)
            def _():
                out_local(v, i).start()

            @pl.when(core != parity)
            def _():
                out_share(v, i).start()

    state = dict(pair=0)
    later = []

    def pass_on(s):
        d, n = order[s]
        z_copy(d, n).wait_recv()
        x_copy(d, n).start()
        if s + ahead < len(order):
            z_copy(*order[s + ahead]).start()

    def pair_step():
        n = state["pair"]
        if n < nc:
            z_copy(1, n).wait_recv()
            if n in at_level[-1]:
                later.append((1, n))
            else:
                x_copy(1, n).start()
            if n + ahead < nc:
                z_copy(1, n + ahead).start()
            state["pair"] = n + 1

    def tokens_1():
        tok_arrival(1, 0).wait_recv()
        for s in range(1, NY):
            tok_copy(1, s).start()
        tok_share(1, 0).start()
        for s in range(1, NY):
            tok_arrival(0, s).wait_recv()
            tok_share(0, s).start()

    def tokens_2():
        for q in range(1, NY):
            tok_arrival(1, q).wait_recv()
            tok_share(1, q).start()

    def tokens_3():
        tok_local.wait()
        for g in range(2):
            for q in range(NY):
                tok_shared(g, q).wait_recv()

    steps = len(order)
    starts = [order.index((cut[0], at_level[v][0])) for v in range(L)]
    spread = starts[1] if L > 2 else starts[1] // 2
    head = len(at_level[0]) * len(cut)
    last = cut[-1]
    queue = []

    def at(step, cost, item):
        queue.append((max(step, 0), len(queue), cost, item))

    at(int(T1 * head) - 1, 0, tokens_1)
    at(int(T2 * head) - 1, 0, tokens_2)
    ready = int(T3 * head) - 1
    at(ready, 0, tokens_3)
    for v in range(L):
        there = {d: order.index((d, at_level[v][-1])) for d in cut}
        cost = 2 * per_core[v]
        at(max(ready, starts[max(v - 1, 0)]), cost, functools.partial(near_job, 0, v))
        at(max(ready, at_level[v][-1]), cost, functools.partial(near_job, 1, v))
        if v == L - 1:
            own_there = pair_there = starts[-1] + 1
        else:
            own_there = spread + at_level[v][-1] - at_level[1][0] + LAG if v else 0
            pair_there = at_level[v][-1] + LAG
        at(max(ready, own_there), cost, functools.partial(across_job, 0, v))
        at(max(ready, pair_there), cost, functools.partial(across_job, 1, v))
        for d in cut:
            final = v == L - 1 and d == last
            if not final:
                at(max(ready, there[d]), cost, functools.partial(near_job, d, v))
            if d != last:
                at(max(ready, there[d] + LAG), cost, functools.partial(across_job, d, v))

        def send_sums(v=v):
            if v:
                pl.semaphore_wait(free, 1)
            if v == L - 1:
                near_job(last, v, theirs)
            across_job(last, v, sent)
            if v == L - 1:
                near_job(last, v, ours)
            across_job(last, v, ours)
            for i in range(per_core[v]):
                sums_copy(v, i, 0).start()

        when = max(ready, there[last] + LAG) if v < L - 1 else steps
        at(when, cost, send_sums)
        for group in (1, 0):
            for i in range(per_core[v]):
                at(when + 1, 2, functools.partial(finish, v, i, group))

        def release(v=v):
            for group in range(2):
                for i in range(per_core[v]):
                    sums_copy(v, i, group).wait_send()
            if v < L - 1:
                pl.semaphore_signal(free, inc=1, device_id=sibling, device_id_type=MESH)

        at(when + 1, 0, release)

    queue.sort(key=lambda entry: entry[:2])
    for s in range(steps):
        pass_on(s)
        pair_step()
        if s >= spread:
            for _ in range(min(len(later), 1 if later and parts[later[0][1]][0] < L - 1 else 2)):
                x_copy(*later.pop(0)).start()
        if s + 1 == starts[-1]:
            while state["pair"] < nc:
                pair_step()
            while later:
                x_copy(*later.pop(0)).start()
        budget = 6 if s < starts[-1] else 4
        while queue and queue[0][0] <= s and budget > 0:
            _, _, cost, item = queue.pop(0)
            item()
            budget -= cost
    for entry in queue:
        entry[3]()

    for n in range(nc):
        w_copy(n).wait_send()
        for d in range(NZ):
            x_copy(d, n).wait_send()
            if d:
                z_copy(d, n).wait_send()
    for g in range(2):
        for s in range(NY):
            if g or s:
                tok_copy(g, s).wait_send()
            tok_share(g, s).wait_send()
    for v in range(L):
        for i in range(per_core[v]):
            out_copy(v, i).wait_send()

            @pl.when(core != parity)
            def _(v=v, i=i):
                out_share(v, i).wait_send()

    for chunk in range(lefts[-1]):
        pltpu.make_async_copy(done_part(0, 0, 0), out_place(chunk), o_recv.at[chunk]).wait()


def solution(mesh):
    R, C = mesh.shape["row"], mesh.shape["col"]
    NZ, NY = R // 2, C // 2
    axes = ("row", "col")

    def on_device(tokens, gate_weight, up_weight, tile_mask):
        depth, cols = gate_weight.shape
        row_tiles, col_tiles = depth // TILE, cols // TILE
        tiles = row_tiles * col_tiles
        slots = 5 * tiles // 8
        rows = tokens.shape[0]
        r = lax.axis_index("row")
        core = lax.axis_index("col") % 2
        home = ((r // 2) % 2) == core

        mask_sib = lax.ppermute(tile_mask, axes, [(d, d ^ 1) for d in range(R * C)])
        smem = pl.BlockSpec(memory_space=pltpu.SMEM)
        hbm = pl.BlockSpec(memory_space=pl.ANY)
        place = jnp.arange(tiles)
        place = (place % col_tiles) * row_tiles + place // col_tiles
        upto = (place[None, :] <= place[:, None]).astype(jnp.int32)

        def slot_codes(mask):
            mask = mask.reshape(R, tiles)
            return jnp.where(mask == 1, jnp.sum(mask[:, None, :] * upto[None], axis=2) - 1, -1)

        here = slot_codes(tile_mask)
        match = here[:, None, :] == jnp.arange(slots)[None, :, None]
        corner = jnp.stack([jnp.arange(tiles) // col_tiles, jnp.arange(tiles) % col_tiles])
        order = jnp.sum(jnp.where(match[None], corner[:, None, None, :], 0), axis=3).reshape(-1)
        codes = slot_codes(jnp.where(home, tile_mask, mask_sib)).reshape(-1)

        levels = levels_of(row_tiles, col_tiles, slots)
        L = len(levels)
        sizes = [stop - start for (stop, _), start in zip(levels, [0] + [v for v, _ in levels])]
        chunk_tiles = min(4, levels[0][1] // 2)
        width = chunk_tiles * TILE
        chunks = col_tiles // chunk_tiles
        most = (col_tiles - levels[-2][1]) // (2 * chunk_tiles)
        nc = len(parts_of(levels))
        bf16, f32 = jnp.bfloat16, jnp.float32
        pieces = [pltpu.VMEM((2, size, TILE, TILE), bf16) for size in sizes]
        for _ in range(2 * NZ):
            pieces += [pltpu.VMEM((size, TILE, TILE), bf16) for size in sizes]
        sem = pltpu.SemaphoreType.DMA
        hidden = pl.pallas_call(
            functools.partial(main_kernel, R, C, row_tiles, col_tiles, slots),
            out_shape=jax.ShapeDtypeStruct((rows, cols), bf16),
            in_specs=[smem, smem, hbm, hbm, hbm],
            out_specs=hbm,
            scratch_shapes=pieces + [
                pltpu.VMEM((2 * rows, tokens.shape[1] * C), bf16),
                pltpu.VMEM((chunks, 2 * rows, width), f32),
                pltpu.VMEM((depth, width), bf16),
                pltpu.VMEM((most, 2 * rows, width), f32),
                pltpu.VMEM((chunks // 2, 2 * rows, width), bf16),
                sem((nc,)), sem((nc,)), sem((2,)),
                sem((NZ, nc)), sem((NZ, nc)), sem((NZ, nc)), sem((NZ, nc)),
                sem, sem((2, NY)), sem((2, NY)), sem((2, NY)), sem((2, NY)),
                sem((L, most, 2)), sem((L, most, 2)), sem((chunks // 2,)), sem((chunks // 2,)),
                sem((chunks,)), pltpu.SemaphoreType.REGULAR,
            ],
            compiler_params=pltpu.CompilerParams(
                vmem_limit_bytes=VMEM_LIMIT, collective_id=0, has_side_effects=True),
            cost_estimate=pl.CostEstimate(
                flops=8 * rows * depth * R * cols // 2, bytes_accessed=rows * cols * 2, transcendentals=rows * cols),
            name="main",
        )(codes, order, tokens, gate_weight, up_weight)
        part = pl.BlockSpec((rows // 4, cols), lambda n: (n, 0))
        return pl.pallas_call(
            copy_kernel,
            out_shape=jax.ShapeDtypeStruct((rows, cols), bf16),
            grid=(4,),
            in_specs=[part],
            out_specs=part,
            name="place",
        )(hidden)

    placed = (P("row", "col"), P("row", "col"), P("row", "col"), P(None, "col"))
    return jax.shard_map(
        on_device, mesh=mesh, in_specs=placed, out_specs=P("row", "col"), check_vma=False
    )
```

time: 303 us -> 296 us (0.977)
  Pallas kernels: 297 us -> 290 us
    pallas_call x1, Pallas kernels: 292 us -> 285 us  [on_device(): pl.pallas_call(functools.partial(main_kernel, R, C, row_tiles, col_tiles,...]
where the time goes in v3:
time: 296 us; the launch traced here: 293 us
  Pallas kernels  290 us (98%)
    pallas_call x1, Pallas kernels, on_device(): pl.pallas_call(functools.partial(main_kernel, R, C, row_tiles, col_tiles,...  285 us
  transfers between devices with their start and end apart: 1, of which 1 were waited for; matrix products, arithmetic and copies ran while one was open for 0% of the time, Pallas kernels for 0%

profile of v3, /device:TPU:1, one launch (start us, length us, event | category | flops | bytes accessed | tf_op | source)
XLA Modules:
  0.0 293.2 jit_solution(13889881855387328605)
XLA Ops:
  0.0 0.1 collective-permute-start
  0.1 0.1 compare_convert_fusion
  0.2 0.8 reshape.133
  1.0 0.4 collective-permute-done
  1.4 0.1 eq.42
  1.5 0.1 mul.44
  1.6 0.3 multiply_reduce_fusion
  1.9 0.1 iota_compare_fusion
  2.0 0.3 select_reduce_fusion
  2.3 0.7 reshape.134.order_ref
  3.0 0.6 bitcast_select_fusion.codes_ref
  3.6 284.8 %main.1.in_ref = bf16[512,4096]{1,0:T(8,128)(2,1)} custom-call(s32[1024]{0:T(1024)} %bitcast_select_fusion.codes_ref, s32[1280]{0:T(1024)} %reshape.134.order_ref, bf16[512,1024]{1,0:T(8,128)(2,1)} %tok_in.1, bf16[512,4096]{1,0:T(8,128)(2,1)} %gate_in.1, bf16[512,4096]{1,0:T(8,128)(2,1)} %up_in.1), custom_call_target="tpu_custom_call" | custom-call | flops 34359738368 | bytes 4194304 | tf_op jit(solution)/shard_map/main/pallas_call | solution.py:463
  288.5 4.7 %place.1 = bf16[512,4096]{1,0:T(8,128)(2,1)} custom-call(bf16[512,4096]{1,0:T(8,128)(2,1)} %main.1.in_ref), custom_call_target="tpu_custom_call" | custom-call | tf_op jit(solution)/shard_map/place/pallas_call | solution.py:487
  (5 shorter events, 0.0 us)
Async XLA Ops:
  0.0 1.4 collective-permute-start

commit v4 on v3

--- a/solution.py
+++ b/solution.py
@@ -14,8 +14,22 @@
 MESH = pl.DeviceIdType.MESH
 
 
-def copy_kernel(in_ref, out_ref):
-    out_ref[...] = in_ref[...]
+def copy_kernel(count, in_ref, out_ref, held, in_sem, out_sem):
+    part = in_ref.shape[0] // count
+
+    def read(n):
+        return pltpu.make_async_copy(in_ref.at[pl.ds(n * part, part)], held.at[n], in_sem.at[n])
+
+    def write(n):
+        return pltpu.make_async_copy(held.at[n], out_ref.at[pl.ds(n * part, part)], out_sem.at[n])
+
+    for n in range(count):
+        read(n).start()
+    for n in range(count):
+        read(n).wait()
+        write(n).start()
+    for n in range(count):
+        write(n).wait()
 
 
 def split(total, parts):
@@ -73,26 +87,35 @@
         return pltpu.make_async_remote_copy(
             src_ref=src, dst_ref=dst, send_sem=send, recv_sem=recv, device_id=device, device_id_type=MESH)
 
-    loads = [pltpu.make_async_copy(ref, tok.at[pl.ds(n * depth, depth), pl.ds(0, col_tiles * TILE)], w_load.at[n])
-             for n, ref in enumerate((gate_in, up_in))]
-    for load in loads:
-        load.start()
-    for load in loads:
-        load.wait()
-
-    for v in range(L):
-        def pack_step(s, carry, v=v):
-            n = r * slots + bottoms[v] + s
-            i, j = order_ref[n], order_ref[R * slots + n]
-            cols = pl.ds(j * TILE, TILE)
-            mine_row = (core * row_tiles + i) * TILE
-            other_row = ((1 - core) * row_tiles + i) * TILE
-            own[v][core, s] = tok[pl.ds(mine_row, TILE), cols]
-            other[v][s] = tok[pl.ds(other_row, TILE), cols]
-            return carry
-
-        count = levels[v][0] - bottoms[v]
-        lax.fori_loop(0, count, pack_step, 0, unroll=min(4, count))
+    def load(ref, n):
+        return pltpu.make_async_copy(ref, tok.at[pl.ds(n * depth, depth), pl.ds(0, col_tiles * TILE)], w_load.at[n])
+
+    @pl.when(core == 0)
+    def _():
+        load(up_in, 0).start()
+        load(gate_in, 1).start()
+
+    @pl.when(core == 1)
+    def _():
+        load(gate_in, 0).start()
+        load(up_in, 1).start()
+
+    for kind in range(2):
+        load(gate_in, kind).wait()
+    for kind in range(2):
+        for v in range(L):
+            def pack_step(s, carry, v=v, kind=kind):
+                n = bottoms[v] + s
+                i, j = order_ref[0, r, n], order_ref[1, r, n]
+                tile = tok[pl.ds((kind * row_tiles + i) * TILE, TILE), pl.ds(j * TILE, TILE)]
+                if kind:
+                    own[v][core, s] = tile
+                else:
+                    other[v][s] = tile
+                return carry
+
+            count = levels[v][0] - bottoms[v]
+            lax.fori_loop(0, count, pack_step, 0, unroll=min(4, count))
 
     partners = [sibling, x_pair, (r ^ 2, c ^ 1)]
     partners += [(r ^ (2 * d), c) for d in range(1, NZ)]
@@ -180,7 +203,7 @@
             chunk = place(n)
             for j in range(chunk_tiles):
                 for i in range(row_tiles):
-                    code = codes_ref[(source * row_tiles + i) * col_tiles + chunk * chunk_tiles + j]
+                    code = codes_ref[source, i * col_tiles + chunk * chunk_tiles + j]
                     value = None
                     for u in range(v + 1):
                         size = levels[u][0] - bottoms[u]
@@ -444,8 +467,8 @@
         here = slot_codes(tile_mask)
         match = here[:, None, :] == jnp.arange(slots)[None, :, None]
         corner = jnp.stack([jnp.arange(tiles) // col_tiles, jnp.arange(tiles) % col_tiles])
-        order = jnp.sum(jnp.where(match[None], corner[:, None, None, :], 0), axis=3).reshape(-1)
-        codes = slot_codes(jnp.where(home, tile_mask, mask_sib)).reshape(-1)
+        order = jnp.sum(jnp.where(match[None], corner[:, None, None, :], 0), axis=3)
+        codes = slot_codes(jnp.where(home, tile_mask, mask_sib))
 
         levels = levels_of(row_tiles, col_tiles, slots)
         L = len(levels)
@@ -483,13 +506,13 @@
                 flops=8 * rows * depth * R * cols // 2, bytes_accessed=rows * cols * 2, transcendentals=rows * cols),
             name="main",
         )(codes, order, tokens, gate_weight, up_weight)
-        part = pl.BlockSpec((rows // 4, cols), lambda n: (n, 0))
+        count = 8
         return pl.pallas_call(
-            copy_kernel,
+            functools.partial(copy_kernel, count),
             out_shape=jax.ShapeDtypeStruct((rows, cols), bf16),
-            grid=(4,),
-            in_specs=[part],
-            out_specs=part,
+            in_specs=[hbm],
+            out_specs=hbm,
+            scratch_shapes=[pltpu.VMEM((count, rows // count, cols), bf16), sem((count,)), sem((count,))],
             name="place",
         )(hidden)
 

time: 296 us -> 295 us (level)
  no operation moved by 1% of the time
where the time goes in v4:
time: 295 us; the launch traced here: 292 us
  Pallas kernels  289 us (98%)
    pallas_call x1, Pallas kernels, on_device(): pl.pallas_call(functools.partial(main_kernel, R, C, row_tiles, col_tiles,...  285 us
  transfers between devices with their start and end apart: 1, of which 1 were waited for; matrix products, arithmetic and copies ran while one was open for 0% of the time, Pallas kernels for 0%

profile of v4, /device:TPU:1, one launch (start us, length us, event | category | flops | bytes accessed | tf_op | source)
XLA Modules:
  0.0 292.4 jit_solution(8971976246068489614)
XLA Ops:
  0.0 0.1 collective-permute-start
  0.1 0.1 compare_convert_fusion
  0.2 0.8 reshape.126
  1.0 0.4 collective-permute-done
  1.4 0.1 reshape.125
  1.5 0.3 multiply_reduce_fusion
  1.8 0.6 add_select_fusion
  2.4 0.1 iota_compare_fusion
  2.5 0.9 select_reduce_fusion.order_ref
  3.4 285.2 %main.1.in_ref = bf16[512,4096]{1,0:T(8,128)(2,1)} custom-call(s32[8,128]{1,0:T(8,128)} %get-tuple-element.8.codes_ref, s32[2,8,80]{2,1,0:T(8,128)} %select_reduce_fusion.order_ref, bf16[512,1024]{1,0:T(8,128)(2,1)} %tok_in.1, bf16[512,4096]{1,0:T(8,128)(2,1)} %gate_in.1, bf16[512,4096]{1,0:T(8,128)(2,1)} %up_in.1), custom_call_target="tpu_custom_call" | custom-call | flops 34359738368 | bytes 4194304 | tf_op jit(solution)/shard_map/main/pallas_call | solution.py:486
  288.6 3.6 %place.1 = bf16[512,4096]{1,0:T(8,128)(2,1)} custom-call(bf16[512,4096]{1,0:T(8,128)(2,1)} %main.1.in_ref), custom_call_target="tpu_custom_call" | custom-call | tf_op jit(solution)/shard_map/place/pallas_call | solution.py:510
  (4 shorter events, 0.0 us)
Async XLA Ops:
  0.0 1.4 collective-permute-start

commit v5 on v4

--- a/solution.py
+++ b/solution.py
@@ -178,7 +178,7 @@
         w_copy(n).start()
     for s in range(1, NY):
         tok_copy(0, s).start()
-    cut = [d for d in range(2, NZ, 2)] + [d for d in range(3, NZ, 2)]
+    cut = [d for d in range(3, NZ, 2)] + [d for d in range(2, NZ, 2)]
     order = [(d, n) for v in range(L) for d in cut for n in at_level[v]]
     ahead = AHEAD
     for n in range(nc):

time: 295 us -> 291 us (0.986)
  no operation moved by 1% of the time
where the time goes in v5:
time: 291 us
  Pallas kernels  287 us (99%)
    pallas_call x1, Pallas kernels, on_device(): pl.pallas_call(functools.partial(main_kernel, R, C, row_tiles, col_tiles,...  284 us
  transfers between devices with their start and end apart: 1, of which 1 were waited for; matrix products, arithmetic and copies ran while one was open for 0% of the time, Pallas kernels for 0%

profile of v5, /device:TPU:1, one launch (start us, length us, event | category | flops | bytes accessed | tf_op | source)
XLA Modules:
  0.0 290.8 jit_solution(3357040146806343888)
XLA Ops:
  0.0 0.1 collective-permute-start
  0.1 0.1 compare_convert_fusion
  0.2 0.8 reshape.126
  1.0 0.4 collective-permute-done
  1.4 0.1 reshape.125
  1.5 0.3 multiply_reduce_fusion
  1.8 0.6 add_select_fusion
  2.4 0.1 iota_compare_fusion
  2.5 0.9 select_reduce_fusion.order_ref
  3.4 283.6 %main.1.in_ref = bf16[512,4096]{1,0:T(8,128)(2,1)} custom-call(s32[8,128]{1,0:T(8,128)} %get-tuple-element.8.codes_ref, s32[2,8,80]{2,1,0:T(8,128)} %select_reduce_fusion.order_ref, bf16[512,1024]{1,0:T(8,128)(2,1)} %tok_in.1, bf16[512,4096]{1,0:T(8,128)(2,1)} %gate_in.1, bf16[512,4096]{1,0:T(8,128)(2,1)} %up_in.1), custom_call_target="tpu_custom_call" | custom-call | flops 34359738368 | bytes 4194304 | tf_op jit(solution)/shard_map/main/pallas_call | solution.py:486
  287.0 3.6 %place.1 = bf16[512,4096]{1,0:T(8,128)(2,1)} custom-call(bf16[512,4096]{1,0:T(8,128)(2,1)} %main.1.in_ref), custom_call_target="tpu_custom_call" | custom-call | tf_op jit(solution)/shard_map/place/pallas_call | solution.py:510
  (4 shorter events, 0.0 us)
Async XLA Ops:
  0.0 1.4 collective-permute-start
